TPU v7x, 32 devices: a whole 2x2x4 slice. The times are simulated.
32 devices in a mesh: tables: 4 (over y, core), rows: 8 (over z, x).
Axes of the slice: x: 2, y: 2, z: 4, core: 2. Of those that a mesh axis runs over, the one named last changes fastest.
Arguments:
- tables_in: bfloat16 [1024, 16, 512], P('rows', 'tables')
- in_weight: bfloat16 [2, 512, 1536], replicated, may hold values from -0.25 to 0.25
- query_bias: bfloat16 [2, 512], replicated, may hold values from -1.75 to 1.75
- value_bias: bfloat16 [2, 512], replicated, may hold values from -1.75 to 1.75
- out_weight: bfloat16 [2, 512, 512], replicated, may hold values from -3 to 3
- out_bias: bfloat16 [2, 512], replicated, may hold values from -1.75 to 1.75
- attn_gain: bfloat16 [2, 512], replicated, may hold values from 0.5 to 1.5
- attn_shift: bfloat16 [2, 512], replicated, may hold values from -1.75 to 1.75
- up_weight: bfloat16 [2, 512, 1024], replicated, may hold values from -0.25 to 0.25
- up_bias: bfloat16 [2, 1024], replicated, may hold values from -3 to 3
- down_weight: bfloat16 [2, 1024, 512], replicated, may hold values from -0.1875 to 0.1875
- down_bias: bfloat16 [2, 512], replicated, may hold values from -1.75 to 1.75
- ffn_gain: bfloat16 [2, 512], replicated, may hold values from 0.5 to 1.5
- ffn_shift: bfloat16 [2, 512], replicated, may hold values from -1.75 to 1.75
- cotangent: bfloat16 [1024, 16, 512], P('rows', 'tables'), may hold values from -6 to 6
- lengths: int32 [16], P('tables'), may hold values from 128 to 1024, as said below
- train_counts: int32 [16], P('tables'), may hold values from 1 to 1023, as said below
Outputs:
- activations: float32 [1024, 16, 512], P('rows', 'tables')
- input_grad: float32 [1024, 16, 512], P('rows', 'tables')
- in_weight_grad: float32 [2, 512, 1536], replicated
- query_bias_grad: float32 [2, 512], replicated
- value_bias_grad: float32 [2, 512], replicated
- out_weight_grad: float32 [2, 512, 512], replicated
- out_bias_grad: float32 [2, 512], replicated
- attn_gain_grad: float32 [2, 512], replicated
- attn_shift_grad: float32 [2, 512], replicated
- up_weight_grad: float32 [2, 512, 1024], replicated
- up_bias_grad: float32 [2, 1024], replicated
- down_weight_grad: float32 [2, 1024, 512], replicated
- down_bias_grad: float32 [2, 512], replicated
- ffn_gain_grad: float32 [2, 512], replicated
- ffn_shift_grad: float32 [2, 512], replicated
- root_means: float32 [2, 3], replicated
Inputs may be any that keep to these rules, and one draw needn't show every extreme that they name: `lengths`: in each group of 4 consecutive tables one table, drawn from the seed, has length 1024. `train_counts`: A table's train count is at least a quarter of its length, rounded down, and below its length; the table of length 1024 in each group has more than 896 train rows, and that of the first group has 1023.
All inputs are finite; a program needn't handle non-finite values.
Results may differ from a plain program's by a relative error of at most 0.024.
The roundings to bfloat16 on the way count: a program that leaves them out, or rounds other values in their place, can miss the bound.
Values may be sent and summed in bfloat16 or wider, within the bound.
A program may use at most 448 MiB of HBM per device.

v0:
```python
import jax
import jax.numpy as jnp
from jax import lax
from jax.sharding import PartitionSpec as P

D = 512
HEADS = 4
LAYERS = 2


EPSILON = 1e-05
MASKED = -1e30


def norm_forward(values, gain_row, offsets):
    average = jnp.mean(values, axis=-1, keepdims=True)
    centered = values - average
    variance = jnp.mean(centered * centered, axis=-1, keepdims=True)
    inverse = lax.rsqrt(variance + EPSILON)
    normed = centered * inverse
    return (normed * gain_row + offsets, normed, inverse)


def norm_backward(upstream, normed, inverse, gain_row):
    scaled = upstream * gain_row
    average = jnp.mean(scaled, axis=-1, keepdims=True)
    projection = jnp.mean(scaled * normed, axis=-1, keepdims=True)
    return inverse * (scaled - average - normed * projection)


def gelu_exact(values):
    return jax.nn.gelu(values, approximate=False)


def split_heads(values):
    return values.reshape(values.shape[0], values.shape[1], HEADS, values.shape[2] // HEADS)


def merge_heads(values):
    return values.reshape(values.shape[0], values.shape[1], values.shape[2] * values.shape[3])


def table_scores(queries, key_rows, usable):
    scores = jnp.einsum(
        "ibhe,jbhe->bhij",
        split_heads(queries),
        split_heads(key_rows),
        preferred_element_type=jnp.float32,
    )
    return jnp.where(usable[:, None, None, :], scores, MASKED)


def row_sums(values):
    return jnp.sum(values.astype(jnp.float32), axis=(0, 1))


def per_device(
    tables_in,
    in_weight,
    query_bias,
    value_bias,
    out_weight,
    out_bias,
    attn_gain,
    attn_shift,
    up_weight,
    up_bias,
    down_weight,
    down_bias,
    ffn_gain,
    ffn_shift,
    cotangent,
    lengths,
    train_counts,
):
    local_rows = tables_in.shape[0]
    seq_rows = local_rows * lax.axis_size("rows")
    positions = lax.axis_index("rows") * local_rows + jnp.arange(local_rows, dtype=jnp.int32)
    valid_rows = (positions[:, None] < lengths[None, :]).astype(jnp.float32)
    valid_cells = valid_rows[:, :, None]
    usable = jnp.arange(seq_rows, dtype=jnp.int32)[None, :] < train_counts[:, None]
    score_scale = (D // HEADS) ** (-0.5)
    column_scale = jnp.concatenate(
        [jnp.full((D,), score_scale, jnp.float32), jnp.ones((2 * D,), jnp.float32)]
    )
    stream = tables_in.astype(jnp.float32)
    stored = []
    squares = []
    for layer_index in range(LAYERS):
        in_low = stream.astype(jnp.bfloat16)
        projected = jnp.einsum(
            "ibd,de->ibe", in_low, in_weight[layer_index], preferred_element_type=jnp.float32
        )
        queries = ((projected[:, :, :D] + query_bias[layer_index]) * score_scale).astype(
            jnp.bfloat16
        )
        key_rows = projected[:, :, D : 2 * D].astype(jnp.bfloat16)
        value_rows = (projected[:, :, 2 * D :] + value_bias[layer_index]).astype(jnp.bfloat16)
        all_keys, all_values = (
            lax.all_gather(key_rows, "rows", axis=0, tiled=True),
            lax.all_gather(value_rows, "rows", axis=0, tiled=True),
        )
        scores = table_scores(queries, all_keys, usable)
        row_max = jnp.max(scores, axis=-1, keepdims=True)
        exponent = jnp.exp(scores - row_max)
        row_total = jnp.sum(exponent, axis=-1, keepdims=True)
        probs_low = (exponent / row_total).astype(jnp.bfloat16)
        log_total = (row_max + jnp.log(row_total))[..., 0]
        attended = merge_heads(
            jnp.einsum(
                "bhij,jbhe->ibhe",
                probs_low,
                split_heads(all_values),
                preferred_element_type=jnp.float32,
            )
        ).astype(jnp.bfloat16)
        branch = (
            jnp.einsum(
                "ibd,de->ibe", attended, out_weight[layer_index], preferred_element_type=jnp.float32
            )
            + out_bias[layer_index]
        )
        first_out, first_norm, first_inverse = norm_forward(
            stream + branch, attn_gain[layer_index], attn_shift[layer_index]
        )
        mid_low = first_out.astype(jnp.bfloat16)
        hidden = (
            jnp.einsum(
                "ibd,df->ibf", mid_low, up_weight[layer_index], preferred_element_type=jnp.float32
            )
            + up_bias[layer_index]
        )
        act_low = gelu_exact(hidden).astype(jnp.bfloat16)
        ffn_out = (
            jnp.einsum(
                "ibf,fd->ibd", act_low, down_weight[layer_index], preferred_element_type=jnp.float32
            )
            + down_bias[layer_index]
        )
        second_out, second_norm, second_inverse = norm_forward(
            first_out + ffn_out, ffn_gain[layer_index], ffn_shift[layer_index]
        )
        squares.append(
            jnp.stack(
                [
                    jnp.sum(valid_cells * stream * stream),
                    jnp.sum(valid_cells * branch * branch),
                    jnp.sum(valid_cells * ffn_out * ffn_out),
                ]
            )
        )
        gathered = (all_keys, all_values)
        stored.append(
            (
                in_low,
                queries,
                key_rows,
                value_rows,
                gathered,
                log_total,
                attended,
                first_norm,
                first_inverse,
                mid_low,
                hidden,
                act_low,
                second_norm,
                second_inverse,
            )
        )
        stream = second_out
    activations = stream * valid_cells
    upstream = cotangent.astype(jnp.float32) * valid_cells
    layer_grads = [None] * LAYERS
    for layer_index in reversed(range(LAYERS)):
        (
            in_low,
            queries,
            key_rows,
            value_rows,
            gathered,
            log_total,
            attended,
            first_norm,
            first_inverse,
            mid_low,
            hidden,
            act_low,
            second_norm,
            second_inverse,
        ) = stored[layer_index]
        ffn_gain_grad = jnp.sum(upstream * second_norm, axis=(0, 1))
        ffn_shift_grad = jnp.sum(upstream, axis=(0, 1))
        second_grad = norm_backward(upstream, second_norm, second_inverse, ffn_gain[layer_index])
        ffn_low = second_grad.astype(jnp.bfloat16)
        down_weight_grad = jnp.einsum(
            "ibf,ibd->fd", act_low, ffn_low, preferred_element_type=jnp.float32
        )
        act_grad = jnp.einsum(
            "ibd,fd->ibf", ffn_low, down_weight[layer_index], preferred_element_type=jnp.float32
        )
        hidden_low = jax.vjp(gelu_exact, hidden)[1](act_grad)[0].astype(jnp.bfloat16)
        up_weight_grad = jnp.einsum(
            "ibd,ibf->df", mid_low, hidden_low, preferred_element_type=jnp.float32
        )
        first_grad = second_grad + jnp.einsum(
            "ibf,df->ibd", hidden_low, up_weight[layer_index], preferred_element_type=jnp.float32
        )
        attn_gain_grad = jnp.sum(first_grad * first_norm, axis=(0, 1))
        attn_shift_grad = jnp.sum(first_grad, axis=(0, 1))
        residual_grad = norm_backward(first_grad, first_norm, first_inverse, attn_gain[layer_index])
        branch_low = residual_grad.astype(jnp.bfloat16)
        out_weight_grad = jnp.einsum(
            "ibd,ibe->de", attended, branch_low, preferred_element_type=jnp.float32
        )
        attended_low = jnp.einsum(
            "ibe,de->ibd", branch_low, out_weight[layer_index], preferred_element_type=jnp.float32
        ).astype(jnp.bfloat16)
        all_keys, all_values = gathered
        scores = table_scores(queries, all_keys, usable)
        attn_probs = jnp.exp(scores - log_total[..., None])
        probs_low = attn_probs.astype(jnp.bfloat16)
        probs_grad = jnp.einsum(
            "ibhe,jbhe->bhij",
            split_heads(attended_low),
            split_heads(all_values),
            preferred_element_type=jnp.float32,
        )
        center = jnp.sum(attn_probs * probs_grad, axis=-1)
        scores_low = (attn_probs * (probs_grad - center[..., None])).astype(jnp.bfloat16)
        query_low = merge_heads(
            jnp.einsum(
                "bhij,jbhe->ibhe",
                scores_low,
                split_heads(all_keys),
                preferred_element_type=jnp.float32,
            )
        ).astype(jnp.bfloat16)
        key_part = jnp.einsum(
            "bhij,ibhe->jbhe", scores_low, split_heads(queries), preferred_element_type=jnp.float32
        )
        value_part = jnp.einsum(
            "bhij,ibhe->jbhe",
            probs_low,
            split_heads(attended_low),
            preferred_element_type=jnp.float32,
        )
        key_sums = lax.psum_scatter(
            jnp.concatenate([merge_heads(key_part), merge_heads(value_part)], axis=-1).astype(
                jnp.bfloat16
            ),
            "rows",
            scatter_dimension=0,
            tiled=True,
        )
        proj_low = jnp.concatenate([query_low, key_sums], axis=-1)
        in_weight_grad = (
            jnp.einsum("ibd,ibe->de", in_low, proj_low, preferred_element_type=jnp.float32)
            * column_scale
        )
        query_bias_grad = row_sums(query_low) * score_scale
        value_bias_grad = row_sums(proj_low[:, :, 2 * D :])
        weight_now = in_weight[layer_index]
        query_input = (
            jnp.einsum(
                "ibe,de->ibd", query_low, weight_now[:, :D], preferred_element_type=jnp.float32
            )
            * score_scale
        )
        other_input = jnp.einsum(
            "ibe,de->ibd", proj_low[:, :, D:], weight_now[:, D:], preferred_element_type=jnp.float32
        )
        upstream = residual_grad + query_input + other_input
        layer_grads[layer_index] = (
            in_weight_grad,
            query_bias_grad,
            value_bias_grad,
            out_weight_grad,
            row_sums(branch_low),
            attn_gain_grad,
            attn_shift_grad,
            up_weight_grad,
            row_sums(hidden_low),
            down_weight_grad,
            row_sums(ffn_low),
            ffn_gain_grad,
            ffn_shift_grad,
        )
    stacked = [
        jnp.stack([layer_grads[layer_index][member] for layer_index in range(LAYERS)])
        for member in range(13)
    ]
    totals = lax.psum(
        (
            stacked[0],
            stacked[1],
            stacked[2],
            stacked[3],
            stacked[4],
            stacked[5],
            stacked[6],
            stacked[7],
            stacked[8],
            stacked[9],
            stacked[10],
            stacked[11],
            stacked[12],
            jnp.stack(squares),
            jnp.sum(valid_rows),
        ),
        ("tables", "rows"),
    )
    root_means = jnp.sqrt(totals[13] / (totals[14] * D))
    return (
        activations,
        upstream,
        totals[0],
        totals[1],
        totals[2],
        totals[3],
        totals[4],
        totals[5],
        totals[6],
        totals[7],
        totals[8],
        totals[9],
        totals[10],
        totals[11],
        totals[12],
        root_means,
    )


def solution(mesh):
    placed = (
        P("rows", "tables", None),
        P(),
        P(),
        P(),
        P(),
        P(),
        P(),
        P(),
        P(),
        P(),
        P(),
        P(),
        P(),
        P(),
        P("rows", "tables", None),
        P("tables"),
        P("tables"),
    )
    return jax.shard_map(
        per_device,
        mesh=mesh,
        in_specs=placed,
        out_specs=(
            P("rows", "tables", None),
            P("rows", "tables", None),
            P(),
            P(),
            P(),
            P(),
            P(),
            P(),
            P(),
            P(),
            P(),
            P(),
            P(),
            P(),
            P(),
            P(),
        ),
        check_vma=False,
    )
```

profile of v0, /device:TPU:0, one launch (start us, length us, event | category | flops | bytes accessed | tf_op | source)
XLA Modules:
  0.0 1064.0 jit_solution(5078091329649975878)
XLA Ops:
  7.2 2.6 fusion.58
  13.8 73.1 %all-gather.7.cloned.1.call-done = bf16[1024,4,512]{2,0,1:T(8,128)(2,1)} async-done(((bf16[128,4,512]{2,0,1:T(8,128)(2,1)}), bf16[1024,4,512]{2,0,1:T(8,128)(2,1)}) %all-gather.7.cloned.1.call-update) | async-done | bytes 4194320 | tf_op jit(solution)/shard_map/all_gather | solution.py:100
  86.9 6.2 copy.124
  93.1 3.7 select_reduce_fusion.1
  96.8 3.2 copy-done
  100.0 1.8 fusion
  101.8 59.5 %all-gather.5.cloned.1.call-done = bf16[1024,4,512]{2,0,1:T(8,128)(2,1)} async-done(((bf16[128,4,512]{2,0,1:T(8,128)(2,1)}), bf16[1024,4,512]{2,0,1:T(8,128)(2,1)}) %all-gather.5.cloned.1.call-update) | async-done | bytes 4194320 | tf_op jit(solution)/shard_map/all_gather | solution.py:101
  161.4 7.4 fusion.64
  168.8 1.5 fusion.152
  172.3 5.8 multiply_convert_fusion.3
  178.1 1.8 fusion.149
  181.8 1.7 copy-done.8
  184.6 2.6 fusion.78
  187.7 68.5 %all-gather.11.cloned.1.call-done = bf16[1024,4,512]{2,0,1:T(8,128)(2,1)} async-done(((bf16[128,4,512]{2,0,1:T(8,128)(2,1)}), bf16[1024,4,512]{2,0,1:T(8,128)(2,1)}) %all-gather.11.cloned.1.call-update) | async-done | bytes 4194320 | tf_op jit(solution)/shard_map/all_gather | solution.py:100
  256.2 6.2 copy.126
  262.4 3.7 select_reduce_fusion
  266.1 3.2 copy-done.1
  269.3 1.8 fusion.1
  271.1 59.4 %all-gather.9.cloned.1.call-done = bf16[1024,4,512]{2,0,1:T(8,128)(2,1)} async-done(((bf16[128,4,512]{2,0,1:T(8,128)(2,1)}), bf16[1024,4,512]{2,0,1:T(8,128)(2,1)}) %all-gather.9.cloned.1.call-update) | async-done | bytes 4194320 | tf_op jit(solution)/shard_map/all_gather | solution.py:101
  330.5 7.4 fusion.67
  338.0 1.6 fusion.147
  341.5 5.1 multiply_convert_fusion.2
  346.6 1.8 fusion.144
  349.4 1.6 convert_reduce_fusion.2
  357.3 2.1 copy.127
  359.3 7.5 fusion.32
  366.9 6.2 copy.88
  373.1 7.7 multiply_reduce_fusion.1
  380.8 4.6 multiply_convert_fusion.1
  385.4 3.3 convolution_convert_fusion.1
  388.8 6.2 copy.87
  395.0 7.8 pad_maximum_fusion
  403.3 3.5 slice_bitcast_fusion.1
  406.8 4.8 convert_reduce_fusion.8
  412.4 1.7 fusion.63
  414.1 136.5 %reduce-scatter.5.cloned.1.call-done = bf16[128,4,1024]{2,0,1:T(8,128)(2,1)} async-done(((bf16[1024,4,1024]{2,0,1:T(8,128)(2,1)}), bf16[128,4,1024]{2,0,1:T(8,128)(2,1)}) %reduce-scatter.5.cloned.1.call-update) | async-done | bytes 1048592 | tf_op jit(solution)/shard_map/reduce_scatter | solution.py:248
  550.6 5.7 multiply_reduce_fusion.3
  564.4 2.0 copy.128
  566.4 7.6 fusion.35
  574.1 7.8 multiply_reduce_fusion
  581.9 2.0 multiply_convert_fusion
  584.0 3.3 convolution_convert_fusion
  587.3 7.7 pad_maximum_fusion.1
  595.0 11.3 %copy.121 = bf16[1024,4096]{1,0:T(8,128)(2,1)} copy(bf16[1024,4096]{0,1:T(8,128)(2,1)} %bitcast.279) | data formatting | bytes 16777216
  606.3 2.0 copy.97
  608.3 1.8 convolution_bitcast_fusion.6
  615.5 2.3 pad_maximum_fusion.3
  618.6 2.6 pad_maximum_fusion.4
  621.2 2.9 fusion.29
  626.7 127.7 %reduce-scatter.7.cloned.1.call-done = bf16[128,4096]{1,0:T(8,128)(2,1)} async-done(((bf16[1024,4096]{1,0:T(8,128)(2,1)}), bf16[128,4096]{1,0:T(8,128)(2,1)}) %reduce-scatter.7.cloned.1.call-update) | async-done | bytes 1048592
  754.4 1.6 copy.122
  758.0 3.4 pad_maximum_fusion.2
  762.6 1.6 copy.104
  764.2 2.0 maximum_bitcast_fusion.1
  766.3 2.0 maximum_bitcast_fusion
  769.6 1.8 fusion.62
  772.2 1.6 copy.105
  774.0 42.2 %all-reduce = (f32[2,512]{1,0:T(2,128)}, f32[2,512]{1,0:T(2,128)}, f32[2,512]{1,0:T(2,128)}, f32[2,512]{1,0:T(2,128)}, f32[2,512]{1,0:T(2,128)}, /*index=5*/f32[...) all-reduce(f32[2,512]{1,0:T(2,128)S(1)} %pad_maximum_fusion.7, ...), channel_id=1, replica_groups=mesh['tables'=4,'rows'=8] {'tables','rows'}, use_global_device_ids=true, to_apply=%region_27.28 | all-reduce | flops 10247 | bytes 81976 | tf_op jit(solution)/shard_map/psum | solution.py:293
  817.4 224.2 %all-reduce.4.cloned.1.call-done = (f32[2,512,1536]{1,2,0:T(8,128)}, f32[2,512,512]{2,1,0:T(8,128)}, f32[2,512,1024]{2,1,0:T(8,128)}, f32[2,1024,512]{2,1,0:T(8,128)}) async-done(((f32[2,512,1536]{1,2,0:T(8,128)}, f32[2,512,512]{2,1,0:T(8,128)}, f32[2,512,1024]{2,1,0:T(8,128)}, f32[2,1024,512]{2,1,0:T(8,128)}), (f32[2,512,1536]{1,2,0:T(8,128)}, f32[2,512,512]{2,1,0:T(8,128)}, f32[2,512,1024]{2,1,0:T(8,128)}, ...) | async-done | bytes 16777232 | tf_op jit(solution)/shard_map/psum | solution.py:293
  1041.6 6.7 copy.106
  1049.6 1.6 copy-done.18
  1051.3 2.1 copy.174
  1053.4 1.6 copy-done.17
  1055.0 2.0 copy.175
  (239 shorter events, 43.7 us)
Async XLA Ops:
  7.2 3.6 copy-start.57
  7.2 3.6 copy-start.58
  7.2 79.7 %all-gather.7.cloned.1.call-start = ((), (), s32[]{:S(2)}) async-start(), calls=%async_computation.3 | async-start | bytes 4718592 | tf_op jit(solution)/shard_map/all_gather | solution.py:100
  10.7 150.7 %all-gather.5.cloned.1.call-start = ((), (), s32[]{:S(2)}) async-start(), calls=%async_computation.2 | async-start | bytes 4718592 | tf_op jit(solution)/shard_map/all_gather | solution.py:101
  10.8 2.7 copy-start.65
  10.8 2.8 copy-start.59
  10.8 2.8 copy-start.60
  10.8 2.8 copy-start.61
  10.8 2.8 copy-start.62
  10.9 2.9 copy-start.63
  10.9 2.9 copy-start.64
  10.9 2.9 copy-start.56
  12.2 244.0 %all-gather.11.cloned.1.call-start = ((), (), s32[]{:S(2)}) async-start(), calls=%async_computation.5 | async-start | bytes 4718592 | tf_op jit(solution)/shard_map/all_gather | solution.py:100
  13.5 79.6 %copy-start.11 = (bf16[128,4,512]{0,2,1:T(8,128)(2,1)}, bf16[128,4,512]{0,2,1:T(8,128)(2,1)S(1)}, u32[]{:S(2)}) copy-start(bf16[128,4,512]{0,2,1:T(8,128)(2,1)S(1)} %copy.123) | copy-start | bytes 1572868
  96.8 3.2 copy-start
  101.8 67.0 %copy-start.37 = (bf16[128,4,512]{2,1,0:T(4,128)(2,1)S(1)}, bf16[128,4,512]{2,1,0:T(4,128)(2,1)}, u32[]{:S(2)}) copy-start(bf16[128,4,512]{2,1,0:T(4,128)(2,1)} %param.17) | copy-start | bytes 1572868
  101.8 67.0 %copy-start.47 = (bf16[2,512,512]{2,1,0:T(8,128)(2,1)S(1)}, bf16[2,512,512]{2,1,0:T(8,128)(2,1)}, u32[]{:S(2)}) copy-start(bf16[2,512,512]{2,1,0:T(8,128)(2,1)} %param.21) | copy-start | bytes 3145732
  168.7 1.8 copy-start.45
  168.8 2.1 copy-start.70
  172.3 5.8 copy-start.32
  172.3 5.8 copy-start.67
  178.1 1.8 copy-start.19
  178.1 2.6 copy-start.7
  184.4 3.0 copy-start.66
  184.4 146.1 %all-gather.9.cloned.1.call-start = ((), (), s32[]{:S(2)}) async-start(), calls=%async_computation.4 | async-start | bytes 4718592 | tf_op jit(solution)/shard_map/all_gather | solution.py:101
  187.3 363.3 %reduce-scatter.5.cloned.1.call-start = ((), (), s32[]{:S(2)}) async-start(), calls=%async_computation.6 | async-start | bytes 9437184 | tf_op jit(solution)/shard_map/reduce_scatter | solution.py:248
  187.7 74.7 %copy-start.13 = (bf16[128,4,512]{0,2,1:T(8,128)(2,1)}, bf16[128,4,512]{0,2,1:T(8,128)(2,1)S(1)}, u32[]{:S(2)}) copy-start(bf16[128,4,512]{0,2,1:T(8,128)(2,1)S(1)} %copy.125) | copy-start | bytes 1572868
  266.1 3.2 copy-start.1
  330.5 7.5 copy-start.48
  338.0 2.2 copy-start.71
  341.5 5.1 copy-start.68
  346.6 1.9 copy-start.21
  346.6 2.1 copy-start.36
  380.8 4.6 copy-start.14
  385.4 3.4 copy-start.4
  402.8 351.6 %reduce-scatter.7.cloned.1.call-start = ((), (), s32[]{:S(2)}) async-start(), calls=%async_computation.7 | async-start | bytes 9437184
  403.3 3.5 copy-start.5
  406.8 4.8 copy-start.29
  406.8 5.6 copy-start.26
  550.6 6.1 copy-start.34
  550.6 6.1 copy-start.69
  556.7 2.8 copy-start.30
  560.9 2.2 copy-start.49
  566.4 7.7 copy-start.15
  566.4 15.5 %slice-start = ((s8[8388608]{0:T(1024)(128)(4,1)}), s8[4194304]{0:T(1024)(128)(4,1)S(1)}, s32[]{:S(2)}) async-start(s8[8388608]{0:T(1024)(128)(4,1)} %bitcast.273), calls=%async_computation.9 | async-start | bytes 8388608
  574.1 7.8 slice-start.1
  581.9 2.0 copy-start.12
  584.0 3.3 copy-start.2
  606.2 435.4 %all-reduce.4.cloned.1.call-start = ((), (), s32[]{:S(2)}) async-start(), calls=%async_computation.8 | async-start | bytes 33554432 | tf_op jit(solution)/shard_map/psum | solution.py:293
  615.5 2.3 copy-start.20
  615.5 2.3 copy-start.31
  618.6 2.6 copy-start.54
  618.6 2.6 copy-start.55
  618.6 2.6 copy-start.73
  618.6 5.5 copy-start.6
  621.2 4.1 copy-start.3
  626.7 130.4 %copy-start.27 = (bf16[4,4,128,128]{3,2,1,0:T(8,128)(2,1)}, bf16[4,4,128,128]{3,2,1,0:T(8,128)(2,1)S(1)}, u32[]{:S(2)}) copy-start(bf16[4,4,128,128]{3,2,1,0:T(8,128)(2,1)S(1)} %get-tuple-element.154) | copy-start | bytes 1572868
  626.7 129.4 %copy-start.38 = (bf16[128,4,512]{2,1,0:T(4,128)(2,1)S(1)}, bf16[128,4,512]{2,1,0:T(4,128)(2,1)}, u32[]{:S(2)}) copy-start(bf16[128,4,512]{2,1,0:T(4,128)(2,1)} %param.17) | copy-start | bytes 1572868
  756.1 1.9 copy-start.28
  761.4 8.2 copy-start.10
  761.4 8.2 copy-start.24
  1041.6 6.7 copy-start.35
  1048.3 2.9 copy-start.18
  1051.3 3.7 copy-start.17
  (19 other events, 25.2 us)
Sparse Core Ops, SparseCore 0:
  10.8 76.0 all-gather.6
  89.7 71.6 all-gather.4
  184.5 71.6 all-gather.10
  258.8 71.6 all-gather.8
  402.9 147.6 reduce-scatter.4
  606.4 148.0 reduce-scatter.6
  761.5 280.0 all-reduce.3
where the time goes:
time: 1080 us; the launch traced here: 1060 us
  waiting for transfers between devices  749 us (69%)
  matrix products  106 us (10%)
  local copies, waits for them, and re-layouts  88.1 us (8%)
  other arithmetic  61.5 us (6%)
  blocking collectives  42.2 us (4%)
  between operations  16.1 us (1%)
    psum x1, waiting for transfers between devices, per_device(): lax.psum((stacked[0], stacked[1], stacked[2], stacked[3], stacked[4], sta...  224 us
    all_gather x2, waiting for transfers between devices, per_device(): lax.all_gather(key_rows, 'rows', axis=0, tiled=True)  142 us
    reduce_scatter x1, waiting for transfers between devices, per_device(): lax.psum_scatter(jnp.concatenate([merge_heads(key_part), merge_heads(valu...  136 us
    unnamed x8, waiting for transfers between devices  128 us
    all_gather x2, waiting for transfers between devices, per_device(): lax.all_gather(value_rows, 'rows', axis=0, tiled=True)  119 us
    unnamed x160, local copies, waits for them, and re-layouts  50.4 us
    psum x1, blocking collectives, per_device(): lax.psum((stacked[0], stacked[1], stacked[2], stacked[3], stacked[4], sta...  42.2 us
  transfers between devices with their start and end apart: 7, of which 7 were waited for; matrix products, arithmetic and copies ran while one was open for 7% of the time, Pallas kernels for 0%

commit v1 on v0

--- a/solution.py
+++ b/solution.py
@@ -1,6 +1,10 @@
+import functools
+
 import jax
 import jax.numpy as jnp
 from jax import lax
+from jax.experimental import pallas as pl
+from jax.experimental.pallas import tpu as pltpu
 from jax.sharding import PartitionSpec as P
 
 D = 512
@@ -54,7 +58,7 @@
     return jnp.sum(values.astype(jnp.float32), axis=(0, 1))
 
 
-def per_device(
+def gathered_device(
     tables_in,
     in_weight,
     query_bias,
@@ -331,6 +335,572 @@
     )
 
 
+MESH = pl.DeviceIdType.MESH
+NT = (((1,), (1,)), ((), ()))
+NN = (((1,), (0,)), ((), ()))
+TN = (((0,), (0,)), ((), ()))
+TILE = 256
+VECTORS = 9
+
+
+def dot(left, right, dims=NN):
+    return lax.dot_general(left, right, dims, preferred_element_type=jnp.float32)
+
+
+def column_sum(values):
+    return jnp.sum(values, axis=0, keepdims=True)
+
+
+def row_mean(values):
+    return jnp.mean(values, axis=-1, keepdims=True)
+
+
+def table_kernel(
+    local,
+    block_tables,
+    seq,
+    x_hbm,
+    cot_hbm,
+    meta_ref,
+    w_in,
+    w_out,
+    w_up,
+    w_down,
+    vectors,
+    act_hbm,
+    xgrad_hbm,
+    g_in,
+    g_out,
+    g_up,
+    g_down,
+    small,
+    in_low,
+    cot_low,
+    stream,
+    queries,
+    kv,
+    attended,
+    stats,
+    norm1,
+    inverse1,
+    mid_low,
+    slope,
+    act_low,
+    norm2,
+    inverse2,
+    meta,
+    bias_row,
+    bias_col,
+    valid,
+    upstream,
+    ffn_low,
+    hidden_low,
+    branch_low,
+    attended_low,
+    stats_rows,
+    dq_t,
+    dkv_own,
+    dkv_send,
+    dkv_recv,
+    proj_low,
+    staged,
+    x_send,
+    x_recv,
+    cot_send,
+    cot_recv,
+    act_send,
+    act_recv,
+    xg_send,
+    xg_recv,
+    local_sem,
+    kv_sem,
+    dkv_sem,
+    meta_sem,
+):
+    rows = block_tables * local
+    dim = in_low.shape[-1]
+    head_dim = dim // HEADS
+    scale = head_dim**-0.5
+    tiles = rows // TILE
+    t = lax.axis_index("tables")
+    r = lax.axis_index("rows")
+    core = lax.rem(t, 2)
+    side = r // block_tables
+    slot = lax.rem(r, block_tables)
+    peer = (t + 1 - 2 * core, r)
+    own_rows = pl.multiple_of(core * rows, rows)
+    peer_rows = pl.multiple_of((1 - core) * rows, rows)
+
+    def partner(k):
+        return (t - core + side, block_tables * core + k)
+
+    def is_self(k):
+        return jnp.logical_and(core == side, slot == k)
+
+    barrier = pltpu.get_barrier_semaphore()
+    pl.semaphore_signal(barrier, inc=1, device_id=peer, device_id_type=MESH)
+    for k in range(block_tables):
+
+        @pl.when(jnp.logical_not(is_self(k)))
+        def _():
+            pl.semaphore_signal(barrier, inc=1, device_id=partner(k), device_id_type=MESH)
+
+    pl.semaphore_wait(barrier, jnp.where(core == side, block_tables, block_tables + 1))
+
+    def spread(source, target, send_sem, recv_sem, own_sem):
+        def remote(k, at):
+            return pltpu.make_async_remote_copy(
+                src_ref=source(k),
+                dst_ref=target(at),
+                send_sem=send_sem.at[k],
+                recv_sem=recv_sem.at[at],
+                device_id=partner(k),
+                device_id_type=MESH,
+            )
+
+        def kept(k):
+            return pltpu.make_async_copy(source(k), target(k), own_sem)
+
+        def start():
+            for k in range(block_tables):
+
+                @pl.when(is_self(k))
+                def _():
+                    kept(k).start()
+
+                @pl.when(jnp.logical_not(is_self(k)))
+                def _():
+                    remote(k, slot).start()
+
+        def arrive():
+            for k in range(block_tables):
+
+                @pl.when(is_self(k))
+                def _():
+                    kept(k).wait()
+
+                @pl.when(jnp.logical_not(is_self(k)))
+                def _():
+                    remote(k, k).wait_recv()
+
+        def left():
+            for k in range(block_tables):
+
+                @pl.when(jnp.logical_not(is_self(k)))
+                def _():
+                    remote(k, slot).wait_send()
+
+        return start, arrive, left
+
+    def by_table(ref):
+        return lambda k: ref.at[k]
+
+    def by_rows(ref):
+        return lambda k: ref.at[pl.ds(k * local, local)]
+
+    x_start, x_arrive, x_left = spread(by_table(x_hbm), by_rows(in_low.at[0]), x_send, x_recv, local_sem.at[0])
+    cot_start, cot_arrive, cot_left = spread(by_table(cot_hbm), by_rows(cot_low), cot_send, cot_recv, local_sem.at[1])
+    act_start, act_arrive, act_left = spread(by_rows(staged.at[0]), by_table(act_hbm), act_send, act_recv, local_sem.at[2])
+    xg_start, xg_arrive, xg_left = spread(by_rows(staged.at[1]), by_table(xgrad_hbm), xg_send, xg_recv, local_sem.at[3])
+
+    def swap(source, target, sems):
+        return pltpu.make_async_remote_copy(
+            src_ref=source,
+            dst_ref=target,
+            send_sem=sems.at[0],
+            recv_sem=sems.at[1],
+            device_id=peer,
+            device_id_type=MESH,
+        )
+
+    x_start()
+    cot_start()
+    meta_own = pltpu.make_async_copy(meta_ref, meta.at[core], local_sem.at[4])
+    meta_own.start()
+    meta_copy = swap(meta_ref, meta.at[core], meta_sem)
+    meta_copy.start()
+
+    small[...] = jnp.zeros_like(small)
+    meta_own.wait()
+    meta_copy.wait()
+    length = meta[side, pl.ds(slot, 1), :][:, :1]
+    train = meta[side, pl.ds(slot + block_tables, 1), :][:, :1]
+    bias_row[...] = jnp.where(lax.broadcasted_iota(jnp.int32, (1, seq), 1) < train, 0.0, MASKED)
+    bias_col[...] = jnp.where(lax.broadcasted_iota(jnp.int32, (seq, 1), 0) < train, 0.0, MASKED)
+    valid[...] = jnp.where(
+        lax.broadcasted_iota(jnp.int32, (rows, 1), 0) + core * rows < length, 1.0, 0.0
+    )
+    x_arrive()
+
+    def vector(index, layer, width):
+        return vectors[pl.ds(layer * VECTORS + index, 1), pl.ds(0, width)]
+
+    def add_small(layer, index, values):
+        at = (pl.ds(layer * 16 + index, 1), pl.ds(0, values.shape[-1]))
+        small[at] = small[at] + values
+
+    def each_tile(body):
+        def step(i, carry):
+            body(pl.ds(pl.multiple_of(i * TILE, TILE), TILE))
+            return carry
+
+        lax.fori_loop(0, tiles, step, 0)
+
+    def head_cols(h):
+        return pl.ds(pl.multiple_of(h * head_dim, head_dim), head_dim)
+
+    def forward(layer):
+        def project(at):
+            projected = dot(in_low[layer, at, :], w_in[layer])
+            queries[layer, at, :] = (
+                (projected[:, :dim] + vector(0, layer, dim)) * scale
+            ).astype(jnp.bfloat16)
+            own = pl.ds(pl.multiple_of(own_rows + at.start, TILE), TILE)
+            kv[layer, own, pl.ds(0, dim)] = projected[:, dim : 2 * dim].astype(jnp.bfloat16)
+            kv[layer, own, pl.ds(dim, dim)] = (
+                projected[:, 2 * dim :] + vector(1, layer, dim)
+            ).astype(jnp.bfloat16)
+
+        each_tile(project)
+        mine = kv.at[layer, pl.ds(own_rows, rows)]
+        kv_copy = swap(mine, mine, kv_sem.at[layer])
+        kv_copy.start()
+        kv_copy.wait()
+
+        def attend(step, carry):
+            h = step // tiles
+            at = pl.ds(pl.multiple_of(lax.rem(step, tiles) * TILE, TILE), TILE)
+            cols = head_cols(h)
+            key_rows = kv[layer, :, cols]
+            value_rows = kv[layer, :, pl.ds(pl.multiple_of(dim + h * head_dim, head_dim), head_dim)]
+            scores = dot(queries[layer, at, cols], key_rows, NT) + bias_row[...]
+            row_max = jnp.max(scores, axis=-1, keepdims=True)
+            exponent = jnp.exp(scores - row_max)
+            total = jnp.sum(exponent, axis=-1, keepdims=True)
+            probs = (exponent * (1.0 / total)).astype(jnp.bfloat16)
+            attended[layer, at, cols] = dot(probs, value_rows).astype(jnp.bfloat16)
+            lane = lax.broadcasted_iota(jnp.int32, (TILE, head_dim), 1)
+            kept = jnp.where(h == 0, jnp.zeros((TILE, head_dim), jnp.float32), stats[layer, at, :])
+            stats[layer, at, :] = jnp.where(lane == h, row_max + jnp.log(total), kept)
+            return carry
+
+        lax.fori_loop(0, HEADS * tiles, attend, 0)
+
+        def dense(at):
+            below = in_low[0, at, :].astype(jnp.float32) if layer == 0 else stream[at, :]
+            branch = dot(attended[layer, at, :], w_out[layer]) + vector(2, layer, dim)
+            valid_cells = valid[at, :]
+            add_small(layer, 10, column_sum(below * below * valid_cells))
+            add_small(layer, 11, column_sum(branch * branch * valid_cells))
+            summed = below + branch
+            centered = summed - row_mean(summed)
+            inverse = lax.rsqrt(row_mean(centered * centered) + EPSILON)
+            normed = centered * inverse
+            norm1[layer, at, :] = normed
+            inverse1[layer, at, :] = inverse
+            first_out = normed * vector(3, layer, dim) + vector(4, layer, dim)
+            mid = first_out.astype(jnp.bfloat16)
+            mid_low[layer, at, :] = mid
+            hidden = dot(mid, w_up[layer]) + vector(5, layer, 2 * dim)
+            cdf = 0.5 + 0.5 * lax.erf(hidden * (0.5**0.5))
+            slope[layer, at, :] = cdf + hidden * (
+                jnp.exp(hidden * hidden * -0.5) * 0.3989422804014327
+            )
+            act = (hidden * cdf).astype(jnp.bfloat16)
+            act_low[layer, at, :] = act
+            ffn_out = dot(act, w_down[layer]) + vector(6, layer, dim)
+            add_small(layer, 12, column_sum(ffn_out * ffn_out * valid_cells))
+            summed = first_out + ffn_out
+            centered = summed - row_mean(summed)
+            inverse = lax.rsqrt(row_mean(centered * centered) + EPSILON)
+            normed = centered * inverse
+            norm2[layer, at, :] = normed
+            inverse2[layer, at, :] = inverse
+            out = normed * vector(7, layer, dim) + vector(8, layer, dim)
+            if layer + 1 < LAYERS:
+                stream[at, :] = out
+                in_low[layer + 1, at, :] = out.astype(jnp.bfloat16)
+            else:
+                staged[0, at, :] = (out * valid_cells).astype(jnp.bfloat16)
+
+        each_tile(dense)
+
+    for layer in range(LAYERS):
+        forward(layer)
+    act_start()
+    cot_arrive()
+
+    def backward(layer):
+        def dense(at):
+            if layer == LAYERS - 1:
+                up = cot_low[at, :].astype(jnp.float32) * valid[at, :]
+            else:
+                up = upstream[at, :]
+            normed = norm2[layer, at, :]
+            add_small(layer, 8, column_sum(up * normed))
+            add_small(layer, 9, column_sum(up))
+            scaled = up * vector(7, layer, dim)
+            second = inverse2[layer, at, :] * (
+                scaled - row_mean(scaled) - normed * row_mean(scaled * normed)
+            )
+            ffn = second.astype(jnp.bfloat16)
+            ffn_low[at, :] = ffn
+            add_small(layer, 7, column_sum(ffn.astype(jnp.float32)))
+            hidden = (dot(ffn, w_down[layer], NT) * slope[layer, at, :]).astype(jnp.bfloat16)
+            hidden_low[at, :] = hidden
+            add_small(layer, 6, column_sum(hidden.astype(jnp.float32)))
+            first = second + dot(hidden, w_up[layer], NT)
+            normed = norm1[layer, at, :]
+            add_small(layer, 4, column_sum(first * normed))
+            add_small(layer, 5, column_sum(first))
+            scaled = first * vector(3, layer, dim)
+            residual = inverse1[layer, at, :] * (
+                scaled - row_mean(scaled) - normed * row_mean(scaled * normed)
+            )
+            upstream[at, :] = residual
+            branch = residual.astype(jnp.bfloat16)
+            branch_low[at, :] = branch
+            add_small(layer, 3, column_sum(branch.astype(jnp.float32)))
+            low = dot(branch, w_out[layer], NT).astype(jnp.bfloat16)
+            attended_low[at, :] = low
+            product = low.astype(jnp.float32) * attended[layer, at, :].astype(jnp.float32)
+            lane = lax.broadcasted_iota(jnp.int32, (TILE, head_dim), 1)
+            held = stats[layer, at, :]
+            for h in range(HEADS):
+                center = jnp.sum(product[:, h * head_dim : (h + 1) * head_dim], axis=-1, keepdims=True)
+                held = jnp.where(lane == HEADS + h, center, held)
+            stats_rows[:, at] = jnp.transpose(held)[: 2 * HEADS, :]
+
+        each_tile(dense)
+        g_down[layer] = dot(act_low[layer], ffn_low[...], TN).astype(jnp.bfloat16)
+        g_up[layer] = dot(mid_low[layer], hidden_low[...], TN).astype(jnp.bfloat16)
+        g_out[layer] = dot(attended[layer], branch_low[...], TN).astype(jnp.bfloat16)
+
+        def attend(base, first, keep):
+            def step(i, carry):
+                h = i // tiles
+                j = pl.multiple_of(lax.rem(i, tiles) * TILE, TILE)
+                at = pl.ds(pl.multiple_of(base + j, TILE), TILE)
+                cols = head_cols(h)
+                value_cols = pl.ds(pl.multiple_of(dim + h * head_dim, head_dim), head_dim)
+                key_rows = kv[layer, at, cols]
+                query_rows = queries[layer, :, cols]
+                grads = attended_low[:, cols]
+                probs = jnp.exp(
+                    dot(key_rows, query_rows, NT) + bias_col[at, :] - stats_rows[pl.ds(h, 1), :]
+                )
+                value_part = dot(probs.astype(jnp.bfloat16), grads)
+                probs_grad = dot(kv[layer, at, value_cols], grads, NT)
+                scores_low = (probs * (probs_grad - stats_rows[pl.ds(HEADS + h, 1), :])).astype(
+                    jnp.bfloat16
+                )
+                key_part = dot(scores_low, query_rows)
+                query_part = dot(key_rows, scores_low, TN)
+                if first:
+                    query_part = jnp.where(j == 0, query_part, query_part + dq_t[cols, :])
+                else:
+                    query_part = query_part + dq_t[cols, :]
+                dq_t[cols, :] = query_part
+                keep(pl.ds(j, TILE), cols, key_part)
+                keep(pl.ds(j, TILE), value_cols, value_part)
+                return carry
+
+            lax.fori_loop(0, HEADS * tiles, step, 0)
+
+        def keep_sent(at, cols, part):
+            dkv_send[layer, at, cols] = part.astype(jnp.bfloat16)
+
+        def keep_own(at, cols, part):
+            dkv_own[at, cols] = part
+
+        attend(peer_rows, True, keep_sent)
+        copy = swap(dkv_send.at[layer], dkv_recv.at[layer], dkv_sem.at[layer])
+        copy.start()
+        attend(own_rows, False, keep_own)
+        copy.wait()
+
+        def finish(at):
+            query = jnp.transpose(dq_t[:, at]).astype(jnp.bfloat16)
+            pair = (dkv_own[at, :] + dkv_recv[layer, at, :].astype(jnp.float32)).astype(jnp.bfloat16)
+            proj_low[at, pl.ds(0, dim)] = query
+            proj_low[at, pl.ds(dim, 2 * dim)] = pair
+            add_small(layer, 0, column_sum(query.astype(jnp.float32)) * scale)
+            add_small(layer, 1, column_sum(pair[:, dim:].astype(jnp.float32)))
+            grad = (
+                upstream[at, :]
+                + dot(query, w_in[layer, :, pl.ds(0, dim)], NT) * scale
+                + dot(pair, w_in[layer, :, pl.ds(dim, 2 * dim)], NT)
+            )
+            if layer > 0:
+                upstream[at, :] = grad
+            else:
+                staged[1, at, :] = grad.astype(jnp.bfloat16)
+
+        each_tile(finish)
+        if layer == 0:
+            xg_start()
+        g_in[layer, :, pl.ds(0, dim)] = (
+            dot(in_low[layer], proj_low[:, pl.ds(0, dim)], TN) * scale
+        ).astype(jnp.bfloat16)
+        g_in[layer, :, pl.ds(dim, 2 * dim)] = dot(
+            in_low[layer], proj_low[:, pl.ds(dim, 2 * dim)], TN
+        ).astype(jnp.bfloat16)
+
+    for layer in reversed(range(LAYERS)):
+        backward(layer)
+    act_arrive()
+    xg_arrive()
+    x_left()
+    cot_left()
+    act_left()
+    xg_left()
+
+
+def table_device(tables, row_parts, *operands):
+    (
+        tables_in,
+        in_weight,
+        query_bias,
+        value_bias,
+        out_weight,
+        out_bias,
+        attn_gain,
+        attn_shift,
+        up_weight,
+        up_bias,
+        down_weight,
+        down_bias,
+        ffn_gain,
+        ffn_shift,
+        cotangent,
+        lengths,
+        train_counts,
+    ) = operands
+    local, block_tables, dim = tables_in.shape
+    rows = local * block_tables
+    seq = local * row_parts
+    hidden = up_weight.shape[-1]
+    head_dim = dim // HEADS
+    f32, bf16 = jnp.float32, jnp.bfloat16
+    vectors = jnp.stack(
+        [
+            jnp.pad(v.astype(f32), ((0, 0), (0, hidden - v.shape[-1])))
+            for v in (
+                query_bias,
+                value_bias,
+                out_bias,
+                attn_gain,
+                attn_shift,
+                up_bias,
+                down_bias,
+                ffn_gain,
+                ffn_shift,
+            )
+        ],
+        axis=1,
+    ).reshape(LAYERS * VECTORS, hidden)
+    meta = jnp.broadcast_to(jnp.concatenate([lengths, train_counts])[:, None], (2 * block_tables, 128))
+    vmem = pl.BlockSpec(memory_space=pltpu.VMEM)
+    hbm = pl.BlockSpec(memory_space=pl.ANY)
+    block = (block_tables, local, dim)
+    dma = pltpu.SemaphoreType.DMA
+    act, xgrad, g_in, g_out, g_up, g_down, small = pl.pallas_call(
+        functools.partial(table_kernel, local, block_tables, seq),
+        out_shape=(
+            jax.ShapeDtypeStruct(block, bf16),
+            jax.ShapeDtypeStruct(block, bf16),
+            jax.ShapeDtypeStruct(in_weight.shape, bf16),
+            jax.ShapeDtypeStruct(out_weight.shape, bf16),
+            jax.ShapeDtypeStruct(up_weight.shape, bf16),
+            jax.ShapeDtypeStruct(down_weight.shape, bf16),
+            jax.ShapeDtypeStruct((LAYERS * 16, hidden), f32),
+        ),
+        in_specs=[hbm, hbm] + [vmem] * 6,
+        out_specs=(hbm, hbm) + (vmem,) * 5,
+        scratch_shapes=[
+            pltpu.VMEM((LAYERS, rows, dim), bf16),
+            pltpu.VMEM((rows, dim), bf16),
+            pltpu.VMEM((rows, dim), f32),
+            pltpu.VMEM((LAYERS, rows, dim), bf16),
+            pltpu.VMEM((LAYERS, seq, 2 * dim), bf16),
+            pltpu.VMEM((LAYERS, rows, dim), bf16),
+            pltpu.VMEM((LAYERS, rows, head_dim), f32),
+            pltpu.VMEM((LAYERS, rows, dim), f32),
+            pltpu.VMEM((LAYERS, rows, 1), f32),
+            pltpu.VMEM((LAYERS, rows, dim), bf16),
+            pltpu.VMEM((LAYERS, rows, hidden), f32),
+            pltpu.VMEM((LAYERS, rows, hidden), bf16),
+            pltpu.VMEM((LAYERS, rows, dim), f32),
+            pltpu.VMEM((LAYERS, rows, 1), f32),
+            pltpu.VMEM((2, 2 * block_tables, 128), jnp.int32),
+            pltpu.VMEM((1, seq), f32),
+            pltpu.VMEM((seq, 1), f32),
+            pltpu.VMEM((rows, 1), f32),
+            pltpu.VMEM((rows, dim), f32),
+            pltpu.VMEM((rows, dim), bf16),
+            pltpu.VMEM((rows, hidden), bf16),
+            pltpu.VMEM((rows, dim), bf16),
+            pltpu.VMEM((rows, dim), bf16),
+            pltpu.VMEM((2 * HEADS, rows), f32),
+            pltpu.VMEM((dim, rows), f32),
+            pltpu.VMEM((rows, 2 * dim), f32),
+            pltpu.VMEM((LAYERS, rows, 2 * dim), bf16),
+            pltpu.VMEM((LAYERS, rows, 2 * dim), bf16),
+            pltpu.VMEM((rows, 3 * dim), bf16),
+            pltpu.VMEM((2, rows, dim), bf16),
+        ]
+        + [dma((block_tables,))] * 8
+        + [dma((5,)), dma((LAYERS, 2)), dma((LAYERS, 2)), dma((2,))],
+        compiler_params=pltpu.CompilerParams(
+            collective_id=0, has_side_effects=True, vmem_limit_bytes=62 * 1024 * 1024
+        ),
+    )(
+        jnp.swapaxes(tables_in, 0, 1),
+        jnp.swapaxes(cotangent, 0, 1),
+        meta,
+        in_weight,
+        out_weight,
+        up_weight,
+        down_weight,
+        vectors,
+    )
+    count = jnp.sum(lengths.astype(f32)) / row_parts
+    totals = lax.psum((g_in, g_out, g_up, g_down, small, count), ("tables", "rows"))
+    g_in, g_out, g_up, g_down = [total.astype(f32) for total in totals[:4]]
+    small, count = totals[4:]
+    small = small.reshape(LAYERS, 16, hidden)
+    root_means = jnp.sqrt(jnp.sum(small[:, 10:13, :dim], axis=-1) / (count * dim))
+
+    def widen(values):
+        return jnp.swapaxes(values, 0, 1).astype(f32)
+
+    return (
+        widen(act),
+        widen(xgrad),
+        g_in,
+        small[:, 0, :dim],
+        small[:, 1, :dim],
+        g_out,
+        small[:, 3, :dim],
+        small[:, 4, :dim],
+        small[:, 5, :dim],
+        g_up,
+        small[:, 6],
+        g_down,
+        small[:, 7, :dim],
+        small[:, 8, :dim],
+        small[:, 9, :dim],
+        root_means,
+    )
+
+
+def per_device(tables, row_parts, *operands):
+    local, block_tables, dim = operands[0].shape
+    if tables % 2 == 0 and row_parts == 2 * block_tables and local * row_parts <= 1024:
+        return table_device(tables, row_parts, *operands)
+    return gathered_device(*operands)
+
+
 def solution(mesh):
     placed = (
         P("rows", "tables", None),
@@ -352,7 +922,7 @@
         P("tables"),
     )
     return jax.shard_map(
-        per_device,
+        functools.partial(per_device, mesh.shape["tables"], mesh.shape["rows"]),
         mesh=mesh,
         in_specs=placed,
         out_specs=(

time: 1080 us -> 451 us (0.42); the launches traced: 1060 us -> 450 us
  waiting for transfers between devices: 749 us -> 258 us
  matrix products: 106 us -> 0 us
  Pallas kernels: 0 us -> 91.6 us
  local copies, waits for them, and re-layouts: 88.1 us -> 19.7 us
  other arithmetic: 61.5 us -> 14.1 us
    all_gather x4 -> x0, waiting for transfers between devices: 261 us -> none  [the longest x2 142 us: per_device(): lax.all_gather(key_rows, 'rows', axis=0, tiled=True)]
    reduce_scatter x1 -> x0, waiting for transfers between devices: 136 us -> none  [per_device(): lax.psum_scatter(jnp.concatenate([merge_heads(key_part), merge_heads(valu...]
    unnamed x8 -> x2, waiting for transfers between devices: 128 us -> 0.69 us
    dot_general x38 -> x0, matrix products: 106 us -> none  [the longest x2 15.5 us: per_device(): jnp.einsum('ibhe,jbhe->bhij', split_heads(attended_low), split_heads(all_...]
    pallas_call x0 -> x1, Pallas kernels: none -> 91.6 us  [table_device(): pl.pallas_call(functools.partial(table_kernel, local, block_tables, seq),...]
    unnamed x160 -> x27, local copies, waits for them, and re-layouts: 50.4 us -> 13.4 us
    psum x1 -> x2, waiting for transfers between devices: 224 us -> 257 us  [table_device(): lax.psum((g_in, g_out, g_up, g_down, small, count), ('tables', 'rows'))]
    reshape x8 -> x3, local copies, waits for them, and re-layouts: 30.5 us -> 2.33 us  [the longest x1 1.66 us: table_device(): small = small.reshape(LAYERS, 16, hidden)]
  transfers between devices with their start and end apart: 7 -> 2, of which waited for: 7 -> 2; matrix products, arithmetic and copies ran while one was open for 7% -> 2% of each run, Pallas kernels for 0% -> 0%
where the time goes in v1:
time: 451 us; the launch traced here: 450 us
  waiting for transfers between devices  258 us (57%)
  Pallas kernels  91.6 us (20%)
  blocking collectives  51.5 us (11%)
  local copies, waits for them, and re-layouts  19.7 us (4%)
  between operations  15.4 us (3%)
  other arithmetic  14.1 us (3%)
    psum x2, waiting for transfers between devices, table_device(): lax.psum((g_in, g_out, g_up, g_down, small, count), ('tables', 'rows'))  257 us
    pallas_call x1, Pallas kernels, table_device(): pl.pallas_call(functools.partial(table_kernel, local, block_tables, seq),...  91.6 us
    psum x1, blocking collectives, table_device(): lax.psum((g_in, g_out, g_up, g_down, small, count), ('tables', 'rows'))  51.5 us
    unnamed x27, local copies, waits for them, and re-layouts  13.4 us
    convert_element_type x4, other arithmetic, table_device(): g_in, g_out, g_up, g_down = [total.astype(f32) for total in totals[:4]]  12.3 us
  transfers between devices with their start and end apart: 2, of which 2 were waited for; matrix products, arithmetic and copies ran while one was open for 2% of the time, Pallas kernels for 0%

profile of v1, /device:TPU:0, one launch (start us, length us, event | category | flops | bytes accessed | tf_op | source)
XLA Modules:
  0.0 450.2 jit_solution(5712110171319575072)
XLA Ops:
  7.2 0.0 copy-start.6
  7.2 0.0 copy-start.5
  7.2 0.0 all-reduce.12.cloned.1.call-start
  7.2 0.7 constant_dynamic-update-slice_fusion.8
  7.9 0.7 constant_dynamic-update-slice_fusion.7
  8.6 0.7 constant_dynamic-update-slice_fusion.6
  9.3 0.7 constant_dynamic-update-slice_fusion.5
  10.0 0.7 constant_dynamic-update-slice_fusion.4
  10.7 0.7 constant_dynamic-update-slice_fusion.3
  11.4 0.7 constant_dynamic-update-slice_fusion.2
  12.1 0.7 constant_dynamic-update-slice_fusion.1
  12.8 0.7 constant_dynamic-update-slice_fusion
  13.5 0.7 reshape.45.vectors
  14.1 1.9 copy.54
  16.1 1.9 copy.55
  18.0 0.0 copy-done.6
  18.0 0.0 copy-done.5
  18.0 0.1 pad_add_fusion
  18.1 0.7 broadcast_in_dim.2.meta_ref
  18.7 91.6 %shard_map.288 = (bf16[4,128,512]{2,1,0:T(8,128)(2,1)}, bf16[4,128,512]{2,1,0:T(8,128)(2,1)}, bf16[2,512,1536]{2,1,0:T(8,128)(2,1)}, bf16[2,512,512]{2,1,0:T(8,1...) custom-call(bf16[4,128,512]{2,1,0:T(8,128)(2,1)} %bitcast.48, ...), custom_call_target="tpu_custom_call" | custom-call | tf_op jit(solution)/shard_map/pallas_call | solution.py:807
  110.4 1.7 copy.48
  112.0 0.0 all-reduce.12.cloned.1.call-update
  112.0 0.0 all-reduce.14.cloned.1.call-start
  112.1 0.0 copy-start.3
  112.1 0.0 copy-start.4
  112.1 0.7 all-reduce.14.cloned.1.call-update
  112.8 0.6 convert_reduce_fusion
  114.0 51.5 %psum.47 = f32[]{:T(128)} all-reduce(f32[]{:T(128)S(6)} %div.9), channel_id=1, replica_groups=mesh['tables'=4,'rows'=8] {'tables','rows'}, use_global_device_ids=true, to_apply=%region_7.8 | all-reduce | flops 1 | bytes 8 | tf_op jit(solution)/shard_map/psum | solution.py:868
  165.5 0.0 copy-done.3
  165.5 0.0 copy-done.4
  165.5 0.3 convert_bitcast_fusion
  165.8 1.7 copy.49
  167.5 1.6 copy.50
  169.8 76.4 %all-reduce.12.cloned.1.call-done = f32[2,16,1024]{2,0,1:T(2,128)} async-done(((f32[2,16,1024]{2,0,1:T(2,128)}), f32[2,16,1024]{2,0,1:T(2,128)}) %all-reduce.12.cloned.1.call-update) | async-done | bytes 131088 | tf_op jit(solution)/shard_map/psum | solution.py:868
  246.2 0.8 slice_reduce_fusion
  247.0 0.7 copy.51
  247.7 1.3 slice_bitcast_fusion
  249.0 1.3 slice_bitcast_fusion.1
  250.3 180.7 %all-reduce.14.cloned.1.call-done = (bf16[2,512,1536]{2,1,0:T(8,128)(2,1)}, bf16[2,512,512]{2,1,0:T(8,128)(2,1)}, bf16[2,512,1024]{2,1,0:T(8,128)(2,1)}, bf16[2,1024,512]{2,1,0:T(8,128)(2,1)}) async-done(((bf16[2,512,1536]{2,1,0:T(8,128)(2,1)}, bf16[2,512,512]{2,1,0:T(8,128)(2,1)}, bf16[2,512,1024]{2,1,0:T(8,128)(2,1)}, bf16[2,1024,512]{2,1,0:T(8,128)(2,1)}), (bf16[2,512,1536]{2,1,0:T(8,128)(2,1)}, ...) | async-done | bytes 8388624 | tf_op jit(solution)/shard_map/psum | solution.py:868
  431.1 0.0 copy-start.1
  431.1 5.6 %convert_element_type.49 = f32[2,512,1536]{2,1,0:T(8,128)} convert(bf16[2,512,1536]{2,1,0:T(8,128)(2,1)} %get-tuple-element.78) | non-fusion elementwise | flops 1572864 | bytes 9437184 | tf_op jit(solution)/shard_map/convert_element_type | solution.py:869
  436.7 0.0 copy-done.1
  436.7 0.0 copy-start
  436.7 2.5 convert_element_type.51
  439.2 0.0 copy-done
  439.2 0.0 copy-start.2
  439.2 2.6 convert_element_type.52
  441.8 0.0 copy-done.2
  441.8 1.6 convert_element_type.50
  (2 shorter events, 0.0 us)
Async XLA Ops:
  7.2 10.8 %copy-start.6 = (s32[4]{0:T(128)S(1)}, s32[4]{0:T(128)}, u32[]{:S(2)}) copy-start(s32[4]{0:T(128)} %param.32) | copy-start | bytes 52
  7.2 10.8 %copy-start.5 = (s32[4]{0:T(128)S(1)}, s32[4]{0:T(128)}, u32[]{:S(2)}) copy-start(s32[4]{0:T(128)} %param.33) | copy-start | bytes 52
  7.2 239.0 %all-reduce.12.cloned.1.call-start = ((), (), s32[]{:S(2)}) async-start(), calls=%async_computation | async-start | bytes 262144 | tf_op jit(solution)/shard_map/psum | solution.py:868
  112.0 319.0 %all-reduce.14.cloned.1.call-start = ((), (), s32[]{:S(2)}) async-start(), calls=%async_computation.1 | async-start | bytes 16777216 | tf_op jit(solution)/shard_map/psum | solution.py:868
  112.1 53.5 %copy-start.3 = (bf16[4,128,512]{2,1,0:T(8,128)(2,1)S(1)}, bf16[4,128,512]{2,1,0:T(8,128)(2,1)}, u32[]{:S(2)}) copy-start(bf16[4,128,512]{2,1,0:T(8,128)(2,1)} %get-tuple-element.23) | copy-start | bytes 1572868
  112.1 53.4 %copy-start.4 = (bf16[4,128,512]{2,1,0:T(8,128)(2,1)S(1)}, bf16[4,128,512]{2,1,0:T(8,128)(2,1)}, u32[]{:S(2)}) copy-start(bf16[4,128,512]{2,1,0:T(8,128)(2,1)} %get-tuple-element.24) | copy-start | bytes 1572868
  431.1 5.6 %copy-start.1 = (bf16[2,512,1024]{2,1,0:T(8,128)(2,1)S(1)}, bf16[2,512,1024]{2,1,0:T(8,128)(2,1)}, u32[]{:S(2)}) copy-start(bf16[2,512,1024]{2,1,0:T(8,128)(2,1)} %get-tuple-element.80) | copy-start | bytes 6291460
  436.7 2.5 copy-start
  439.2 2.6 copy-start.2
Sparse Core Ops, SparseCore 0:
  112.2 134.0 all-reduce.11
  252.2 178.7 all-reduce.13

commit v2 on v1

--- a/solution.py
+++ b/solution.py
@@ -341,6 +341,7 @@
 TN = (((0,), (0,)), ((), ()))
 TILE = 256
 VECTORS = 9
+GROUPS = 2
 
 
 def dot(left, right, dims=NN):
@@ -353,6 +354,194 @@
 
 def row_mean(values):
     return jnp.mean(values, axis=-1, keepdims=True)
+
+
+def reduce_job(part, total, recv, sems, halves, z_peers, quarter):
+    rows = part.shape[0]
+    offsets, sizes, copies, back = [0], [rows], [], []
+    for n, (partner, bit) in enumerate(halves):
+        size = sizes[-1] // 2
+        keep = pl.multiple_of(offsets[-1] + bit * size, size)
+        give = pl.multiple_of(offsets[-1] + (1 - bit) * size, size)
+        copies.append(
+            pltpu.make_async_remote_copy(
+                src_ref=part.at[pl.ds(give, size)],
+                dst_ref=recv[n],
+                send_sem=sems.at[0, n],
+                recv_sem=sems.at[1, n],
+                device_id=partner,
+                device_id_type=MESH,
+            )
+        )
+        offsets.append(keep)
+        sizes.append(size)
+        back.append(
+            pltpu.make_async_remote_copy(
+                src_ref=total.at[pl.ds(keep, size)],
+                dst_ref=total.at[pl.ds(keep, size)],
+                send_sem=sems.at[0, 3 + n],
+                recv_sem=sems.at[1, 3 + n],
+                device_id=partner,
+                device_id_type=MESH,
+            )
+        )
+    size = sizes[-1] // (len(z_peers) + 1)
+    base = offsets[-1]
+
+    def piece(index):
+        return pl.ds(pl.multiple_of(base + index * size, size), size)
+
+    mine = piece(quarter)
+    spread, gather = [], []
+    for n, (peer, index) in enumerate(z_peers):
+        spread.append(
+            pltpu.make_async_remote_copy(
+                src_ref=part.at[piece(index)],
+                dst_ref=recv[3].at[n],
+                send_sem=sems.at[0, 6 + n],
+                recv_sem=sems.at[1, 6 + n],
+                device_id=peer,
+                device_id_type=MESH,
+            )
+        )
+        gather.append(
+            pltpu.make_async_remote_copy(
+                src_ref=part.at[mine],
+                dst_ref=total.at[mine],
+                send_sem=sems.at[0, 9 + n],
+                recv_sem=sems.at[1, 9 + n],
+                device_id=peer,
+                device_id_type=MESH,
+            )
+        )
+    kept = pltpu.make_async_copy(part.at[mine], total.at[mine], sems.at[0, 12])
+
+    def add(n):
+        size = sizes[n + 1]
+        step = min(size, 128)
+
+        def chunk(i, carry):
+            start = i * step
+            at = pl.ds(pl.multiple_of(offsets[n + 1] + start, step), step)
+            other = recv[n][pl.ds(pl.multiple_of(start, step), step), :].astype(jnp.float32)
+            part[at, :] = (part[at, :].astype(jnp.float32) + other).astype(part.dtype)
+            return carry
+
+        lax.fori_loop(0, size // step, chunk, 0)
+
+    def first():
+        copies[0].start()
+
+    def fold(n):
+        def run():
+            copies[n].wait()
+            add(n)
+            if n + 1 < len(copies):
+                copies[n + 1].start()
+            else:
+                for copy in spread:
+                    copy.start()
+
+        return run
+
+    def settle():
+        for copy in spread:
+            copy.wait()
+        others = [recv[3][n].astype(jnp.float32) for n in range(len(spread))]
+        own = part[mine, :].astype(jnp.float32)
+        part[mine, :] = ((own + others[0]) + (others[1] + others[2])).astype(part.dtype)
+        kept.start()
+        for copy in gather:
+            copy.start()
+
+    def collect():
+        kept.wait()
+        for copy in gather:
+            copy.wait()
+        back[-1].start()
+
+    def unfold(n):
+        def run():
+            back[n].wait()
+            if n > 0:
+                back[n - 1].start()
+
+        return run
+
+    return [first] + [fold(n) for n in range(3)] + [settle, collect] + [unfold(n) for n in (2, 1, 0)]
+
+
+def small_job(part, total, recv, sems, halves, z_peers):
+    offset, size, copies, back, kept_cols = 0, part.shape[1], [], [], []
+    for n, (partner, bit) in enumerate(halves):
+        size = size // 2
+        keep = pl.ds(pl.multiple_of(offset + bit * size, size), size)
+        give = pl.ds(pl.multiple_of(offset + (1 - bit) * size, size), size)
+        copies.append(
+            pltpu.make_async_remote_copy(
+                src_ref=part.at[:, give],
+                dst_ref=recv[n],
+                send_sem=sems.at[0, n],
+                recv_sem=sems.at[1, n],
+                device_id=partner,
+                device_id_type=MESH,
+            )
+        )
+        back.append(
+            pltpu.make_async_remote_copy(
+                src_ref=total.at[:, keep],
+                dst_ref=total.at[:, keep],
+                send_sem=sems.at[0, 3 + n],
+                recv_sem=sems.at[1, 3 + n],
+                device_id=partner,
+                device_id_type=MESH,
+            )
+        )
+        kept_cols.append(keep)
+        offset = offset + bit * size
+    mine = kept_cols[-1]
+    spread = [
+        pltpu.make_async_remote_copy(
+            src_ref=part.at[:, mine],
+            dst_ref=recv[3].at[n],
+            send_sem=sems.at[0, 6 + n],
+            recv_sem=sems.at[1, 6 + n],
+            device_id=peer,
+            device_id_type=MESH,
+        )
+        for n, (peer, _) in enumerate(z_peers)
+    ]
+
+    def first():
+        copies[0].start()
+
+    def fold(n):
+        def run():
+            copies[n].wait()
+            part[:, kept_cols[n]] = part[:, kept_cols[n]] + recv[n][...]
+            if n + 1 < len(copies):
+                copies[n + 1].start()
+            else:
+                for copy in spread:
+                    copy.start()
+
+        return run
+
+    def settle():
+        for copy in spread:
+            copy.wait()
+        total[:, mine] = (part[:, mine] + recv[3][0]) + (recv[3][1] + recv[3][2])
+        back[-1].start()
+
+    def unfold(n):
+        def run():
+            back[n].wait()
+            if n > 0:
+                back[n - 1].start()
+
+        return run
+
+    return [first] + [fold(n) for n in range(3)] + [settle] + [unfold(n) for n in (2, 1, 0)]
 
 
 def table_kernel(
@@ -362,66 +551,87 @@
     x_hbm,
     cot_hbm,
     meta_ref,
-    w_in,
-    w_out,
-    w_up,
-    w_down,
-    vectors,
-    act_hbm,
-    xgrad_hbm,
-    g_in,
-    g_out,
-    g_up,
-    g_down,
-    small,
-    in_low,
-    cot_low,
-    stream,
-    queries,
-    kv,
-    attended,
-    stats,
-    norm1,
-    inverse1,
-    mid_low,
-    slope,
-    act_low,
-    norm2,
-    inverse2,
-    meta,
-    bias_row,
-    bias_col,
-    valid,
-    upstream,
-    ffn_low,
-    hidden_low,
-    branch_low,
-    attended_low,
-    stats_rows,
-    dq_t,
-    dkv_own,
-    dkv_send,
-    dkv_recv,
-    proj_low,
-    staged,
-    x_send,
-    x_recv,
-    cot_send,
-    cot_recv,
-    act_send,
-    act_recv,
-    xg_send,
-    xg_recv,
-    local_sem,
-    kv_sem,
-    dkv_sem,
-    meta_sem,
+    w_in_hbm,
+    w_out_hbm,
+    w_up_hbm,
+    w_down_hbm,
+    *refs,
 ):
+    vector_refs, refs = refs[:VECTORS], refs[VECTORS:]
+    (
+        act_hbm,
+        xgrad_hbm,
+        t_in,
+        t_out,
+        t_up,
+        t_down,
+        t_small,
+        w_in,
+        w_out,
+        w_up,
+        w_down,
+        vectors,
+        g_in,
+        g_out,
+        g_up,
+        g_down,
+        small,
+        in_low,
+        cot_low,
+        stream,
+        queries,
+        kv,
+        attended,
+        stats,
+        norm1,
+        inverse1,
+        mid_low,
+        slope,
+        act_low,
+        norm2,
+        inverse2,
+        meta,
+        bias_row,
+        bias_col,
+        valid,
+        ffn_low,
+        hidden_low,
+        branch_low,
+        attended_low,
+        stats_rows,
+        dq_t,
+        dkv_own,
+        dkv_send,
+        dkv_recv,
+        proj_low,
+        staged,
+        recv_in,
+        recv_out,
+        recv_up,
+        recv_down,
+        recv_small,
+        x_send,
+        x_recv,
+        cot_send,
+        cot_recv,
+        act_send,
+        act_recv,
+        xg_send,
+        xg_recv,
+        local_sem,
+        kv_sem,
+        dkv_sem,
+        meta_sem,
+        job_sem,
+    ) = refs
+    upstream = stream
     rows = block_tables * local
     dim = in_low.shape[-1]
     head_dim = dim // HEADS
     scale = head_dim**-0.5
     tiles = rows // TILE
+    group_heads = HEADS // GROUPS
+    group_width = group_heads * head_dim
     t = lax.axis_index("tables")
     r = lax.axis_index("rows")
     core = lax.rem(t, 2)
@@ -431,6 +641,31 @@
     own_rows = pl.multiple_of(core * rows, rows)
     peer_rows = pl.multiple_of((1 - core) * rows, rows)
 
+    x_side, y_side, z_side = lax.rem(r, 2), t // 2, r // 2
+    x_next = (t, r + 1 - 2 * x_side)
+    y_next = (t + 2 - 4 * y_side, r)
+    z_next = [
+        (z_side + 1 - 2 * lax.rem(z_side, 2)),
+        lax.rem(z_side + 2, 4),
+        3 - z_side,
+    ]
+    z_peers = [((t, 2 * z + x_side), z) for z in z_next]
+
+    def choose(first, second):
+        return core * second + (1 - core) * first
+
+    halves = [
+        (peer, core),
+        (
+            (choose(x_next[0], y_next[0]), choose(x_next[1], y_next[1])),
+            choose(x_side, y_side),
+        ),
+        (
+            (choose(y_next[0], x_next[0]), choose(y_next[1], x_next[1])),
+            choose(y_side, x_side),
+        ),
+    ]
+
     def partner(k):
         return (t - core + side, block_tables * core + k)
 
@@ -438,14 +673,18 @@
         return jnp.logical_and(core == side, slot == k)
 
     barrier = pltpu.get_barrier_semaphore()
-    pl.semaphore_signal(barrier, inc=1, device_id=peer, device_id_type=MESH)
+    greeted = [peer, x_next, y_next] + [device for device, _ in z_peers]
+    for device in greeted:
+        pl.semaphore_signal(barrier, inc=1, device_id=device, device_id_type=MESH)
     for k in range(block_tables):
 
         @pl.when(jnp.logical_not(is_self(k)))
         def _():
             pl.semaphore_signal(barrier, inc=1, device_id=partner(k), device_id_type=MESH)
 
-    pl.semaphore_wait(barrier, jnp.where(core == side, block_tables, block_tables + 1))
+    pl.semaphore_wait(
+        barrier, len(greeted) + jnp.where(core == side, block_tables - 1, block_tables)
+    )
 
     def spread(source, target, send_sem, recv_sem, own_sem):
         def remote(k, at):
@@ -514,7 +753,20 @@
         )
 
     x_start()
+    loads = [
+        pltpu.make_async_copy(source, target, local_sem.at[5 + n])
+        for n, (source, target) in enumerate(
+            ((w_in_hbm, w_in), (w_out_hbm, w_out), (w_up_hbm, w_up), (w_down_hbm, w_down))
+        )
+    ]
+    for load in loads:
+        load.start()
     cot_start()
+    for n, ref in enumerate(vector_refs):
+        for layer in range(LAYERS):
+            vectors[pl.ds(layer * VECTORS + n, 1), pl.ds(0, ref.shape[1])] = ref[...].astype(
+                jnp.float32
+            )[layer : layer + 1, :]
     meta_own = pltpu.make_async_copy(meta_ref, meta.at[core], local_sem.at[4])
     meta_own.start()
     meta_copy = swap(meta_ref, meta.at[core], meta_sem)
@@ -530,13 +782,15 @@
     valid[...] = jnp.where(
         lax.broadcasted_iota(jnp.int32, (rows, 1), 0) + core * rows < length, 1.0, 0.0
     )
+    small[0, pl.ds(13, 1), pl.ds(0, 128)] = jnp.broadcast_to(column_sum(valid[...]), (1, 128))
     x_arrive()
+    loads[0].wait()
 
     def vector(index, layer, width):
         return vectors[pl.ds(layer * VECTORS + index, 1), pl.ds(0, width)]
 
     def add_small(layer, index, values):
-        at = (pl.ds(layer * 16 + index, 1), pl.ds(0, values.shape[-1]))
+        at = (layer, pl.ds(index, 1), pl.ds(0, values.shape[-1]))
         small[at] = small[at] + values
 
     def each_tile(body):
@@ -585,6 +839,9 @@
             return carry
 
         lax.fori_loop(0, HEADS * tiles, attend, 0)
+        if layer == 0:
+            for load in loads[1:]:
+                load.wait()
 
         def dense(at):
             below = in_low[0, at, :].astype(jnp.float32) if layer == 0 else stream[at, :]
@@ -630,8 +887,27 @@
     act_start()
     cot_arrive()
 
+    jobs = []
+
+    def begin(steps):
+        jobs.append(list(steps))
+        jobs[-1].pop(0)()
+
+    def tick():
+        for steps in jobs:
+            if steps:
+                steps.pop(0)()
+
+    def job(index, part, total, recv):
+        return reduce_job(part, total, recv, job_sem.at[index], halves, z_peers, z_side)
+
     def backward(layer):
-        def dense(at):
+        first_job = (LAYERS - 1 - layer) * 6
+
+        def recv_of(refs):
+            return [ref.at[layer] for ref in refs]
+
+        def enter(at):
             if layer == LAYERS - 1:
                 up = cot_low[at, :].astype(jnp.float32) * valid[at, :]
             else:
@@ -643,13 +919,23 @@
             second = inverse2[layer, at, :] * (
                 scaled - row_mean(scaled) - normed * row_mean(scaled * normed)
             )
+            upstream[at, :] = second
             ffn = second.astype(jnp.bfloat16)
             ffn_low[at, :] = ffn
             add_small(layer, 7, column_sum(ffn.astype(jnp.float32)))
-            hidden = (dot(ffn, w_down[layer], NT) * slope[layer, at, :]).astype(jnp.bfloat16)
+
+        each_tile(enter)
+        g_down[layer] = dot(act_low[layer], ffn_low[...], TN).astype(jnp.bfloat16)
+        tick()
+        begin(job(first_job, g_down.at[layer], t_down.at[layer], recv_of(recv_down)))
+
+        def dense(at):
+            hidden = (dot(ffn_low[at, :], w_down[layer], NT) * slope[layer, at, :]).astype(
+                jnp.bfloat16
+            )
             hidden_low[at, :] = hidden
             add_small(layer, 6, column_sum(hidden.astype(jnp.float32)))
-            first = second + dot(hidden, w_up[layer], NT)
+            first = upstream[at, :] + dot(hidden, w_up[layer], NT)
             normed = norm1[layer, at, :]
             add_small(layer, 4, column_sum(first * normed))
             add_small(layer, 5, column_sum(first))
@@ -672,13 +958,16 @@
             stats_rows[:, at] = jnp.transpose(held)[: 2 * HEADS, :]
 
         each_tile(dense)
-        g_down[layer] = dot(act_low[layer], ffn_low[...], TN).astype(jnp.bfloat16)
+        tick()
         g_up[layer] = dot(mid_low[layer], hidden_low[...], TN).astype(jnp.bfloat16)
+        begin(job(first_job + 1, g_up.at[layer], t_up.at[layer], recv_of(recv_up)))
         g_out[layer] = dot(attended[layer], branch_low[...], TN).astype(jnp.bfloat16)
-
-        def attend(base, first, keep):
+        tick()
+        begin(job(first_job + 2, g_out.at[layer], t_out.at[layer], recv_of(recv_out)))
+
+        def attend(group, base, first, keep):
             def step(i, carry):
-                h = i // tiles
+                h = group * group_heads + i // tiles
                 j = pl.multiple_of(lax.rem(i, tiles) * TILE, TILE)
                 at = pl.ds(pl.multiple_of(base + j, TILE), TILE)
                 cols = head_cols(h)
@@ -701,59 +990,136 @@
                 else:
                     query_part = query_part + dq_t[cols, :]
                 dq_t[cols, :] = query_part
-                keep(pl.ds(j, TILE), cols, key_part)
-                keep(pl.ds(j, TILE), value_cols, value_part)
+                inside = i // tiles * head_dim
+                keep(pl.ds(j, TILE), pl.ds(pl.multiple_of(inside, head_dim), head_dim), key_part)
+                keep(
+                    pl.ds(j, TILE),
+                    pl.ds(pl.multiple_of(group_width + inside, head_dim), head_dim),
+                    value_part,
+                )
                 return carry
 
-            lax.fori_loop(0, HEADS * tiles, step, 0)
-
-        def keep_sent(at, cols, part):
-            dkv_send[layer, at, cols] = part.astype(jnp.bfloat16)
-
-        def keep_own(at, cols, part):
-            dkv_own[at, cols] = part
-
-        attend(peer_rows, True, keep_sent)
-        copy = swap(dkv_send.at[layer], dkv_recv.at[layer], dkv_sem.at[layer])
-        copy.start()
-        attend(own_rows, False, keep_own)
-        copy.wait()
-
-        def finish(at):
-            query = jnp.transpose(dq_t[:, at]).astype(jnp.bfloat16)
-            pair = (dkv_own[at, :] + dkv_recv[layer, at, :].astype(jnp.float32)).astype(jnp.bfloat16)
-            proj_low[at, pl.ds(0, dim)] = query
-            proj_low[at, pl.ds(dim, 2 * dim)] = pair
-            add_small(layer, 0, column_sum(query.astype(jnp.float32)) * scale)
-            add_small(layer, 1, column_sum(pair[:, dim:].astype(jnp.float32)))
-            grad = (
-                upstream[at, :]
-                + dot(query, w_in[layer, :, pl.ds(0, dim)], NT) * scale
-                + dot(pair, w_in[layer, :, pl.ds(dim, 2 * dim)], NT)
-            )
+            lax.fori_loop(0, group_heads * tiles, step, 0)
+
+        for group in range(GROUPS):
+
+            def keep_sent(at, cols, part):
+                dkv_send[layer, group, at, cols] = part.astype(jnp.bfloat16)
+
+            def keep_own(at, cols, part):
+                dkv_own[at, cols] = part
+
+            attend(group, peer_rows, True, keep_sent)
+            copy = swap(
+                dkv_send.at[layer, group], dkv_recv.at[layer, group], dkv_sem.at[layer, group]
+            )
+            copy.start()
+            tick()
+            attend(group, own_rows, False, keep_own)
+            tick()
+            copy.wait()
+
+            def finish(at):
+                group_rows = pl.ds(group * group_width, group_width)
+                query = jnp.transpose(dq_t[group_rows, at]).astype(jnp.bfloat16)
+                pair = (dkv_own[at, :] + dkv_recv[layer, group, at, :].astype(jnp.float32)).astype(
+                    jnp.bfloat16
+                )
+                proj_low[group, at, pl.ds(0, group_width)] = query
+                proj_low[group, at, pl.ds(group_width, 2 * group_width)] = pair
+                cols = pl.ds(group * group_width, group_width)
+                small[layer, pl.ds(0, 1), cols] += column_sum(query.astype(jnp.float32)) * scale
+                small[layer, pl.ds(1, 1), cols] += column_sum(
+                    pair[:, group_width:].astype(jnp.float32)
+                )
+
+            each_tile(finish)
+            grad = dot(in_low[layer], proj_low[group], TN)
+            g_in[layer, group, :, pl.ds(0, group_width)] = (grad[:, :group_width] * scale).astype(
+                jnp.bfloat16
+            )
+            g_in[layer, group, :, pl.ds(group_width, 2 * group_width)] = grad[
+                :, group_width:
+            ].astype(jnp.bfloat16)
+            begin(
+                job(
+                    first_job + 3 + group,
+                    g_in.at[layer, group],
+                    t_in.at[layer, group],
+                    [ref.at[layer, group] for ref in recv_in],
+                )
+            )
+        begin(
+            small_job(
+                small.at[layer],
+                t_small.at[layer],
+                [ref.at[layer] for ref in recv_small],
+                job_sem.at[first_job + 5],
+                halves,
+                z_peers,
+            )
+        )
+
+        def pass_down(at):
+            grad = upstream[at, :]
+            for group in range(GROUPS):
+                for n in range(3):
+                    part = dot(
+                        proj_low[group, at, pl.ds(n * group_width, group_width)],
+                        w_in[layer, :, pl.ds(n * dim + group * group_width, group_width)],
+                        NT,
+                    )
+                    grad = grad + (part * scale if n == 0 else part)
             if layer > 0:
                 upstream[at, :] = grad
             else:
                 staged[1, at, :] = grad.astype(jnp.bfloat16)
 
-        each_tile(finish)
+        each_tile(pass_down)
         if layer == 0:
             xg_start()
-        g_in[layer, :, pl.ds(0, dim)] = (
-            dot(in_low[layer], proj_low[:, pl.ds(0, dim)], TN) * scale
-        ).astype(jnp.bfloat16)
-        g_in[layer, :, pl.ds(dim, 2 * dim)] = dot(
-            in_low[layer], proj_low[:, pl.ds(dim, 2 * dim)], TN
-        ).astype(jnp.bfloat16)
+        tick()
 
     for layer in reversed(range(LAYERS)):
         backward(layer)
+    while any(jobs):
+        tick()
     act_arrive()
     xg_arrive()
     x_left()
     cot_left()
     act_left()
     xg_left()
+
+
+def widen_kernel(f_in, f_out, f_up, f_down, f_act, f_xgrad, small, *outs):
+    act, xgrad, in_weight, out_weight, up_weight, down_weight, root_means = outs[:7]
+    groups, width = f_in.shape[1], f_in.shape[3] // 3
+    for group in range(groups):
+        for n in range(3):
+            in_weight[0, :, pl.ds((n * groups + group) * width, width)] = f_in[
+                0, group, :, pl.ds(n * width, width)
+            ].astype(jnp.float32)
+    out_weight[...] = f_out[...].astype(jnp.float32)
+    up_weight[...] = f_up[...].astype(jnp.float32)
+    down_weight[...] = f_down[...].astype(jnp.float32)
+    for k in range(f_act.shape[0]):
+        act[:, k, :] = f_act[k].astype(jnp.float32)
+        xgrad[:, k, :] = f_xgrad[k].astype(jnp.float32)
+
+    @pl.when(pl.program_id(0) == 0)
+    def _():
+        for ref, row in zip(outs[7:], (0, 1, 3, 4, 5, 6, 7, 8, 9)):
+            for layer in range(LAYERS):
+                ref[pl.ds(layer, 1), :] = small[layer, pl.ds(row, 1), pl.ds(0, ref.shape[1])]
+        dim = f_act.shape[2]
+        count = small[0, pl.ds(13, 1), pl.ds(0, 1)]
+        for layer in range(LAYERS):
+            sums = jnp.sum(small[layer, pl.ds(8, 8), pl.ds(0, dim)], axis=-1, keepdims=True)
+            for n in range(3):
+                root_means[pl.ds(layer, 1), pl.ds(n, 1)] = jnp.sqrt(
+                    sums[2 + n : 3 + n, :] / (count * dim)
+                )
 
 
 def table_device(tables, row_parts, *operands):
@@ -782,42 +1148,46 @@
     hidden = up_weight.shape[-1]
     head_dim = dim // HEADS
     f32, bf16 = jnp.float32, jnp.bfloat16
-    vectors = jnp.stack(
-        [
-            jnp.pad(v.astype(f32), ((0, 0), (0, hidden - v.shape[-1])))
-            for v in (
-                query_bias,
-                value_bias,
-                out_bias,
-                attn_gain,
-                attn_shift,
-                up_bias,
-                down_bias,
-                ffn_gain,
-                ffn_shift,
-            )
-        ],
-        axis=1,
-    ).reshape(LAYERS * VECTORS, hidden)
+    groups = GROUPS
     meta = jnp.broadcast_to(jnp.concatenate([lengths, train_counts])[:, None], (2 * block_tables, 128))
     vmem = pl.BlockSpec(memory_space=pltpu.VMEM)
     hbm = pl.BlockSpec(memory_space=pl.ANY)
     block = (block_tables, local, dim)
     dma = pltpu.SemaphoreType.DMA
-    act, xgrad, g_in, g_out, g_up, g_down, small = pl.pallas_call(
+    in_part = (LAYERS, groups, dim, 3 * dim // groups)
+    shards = 8 * row_parts // 2
+
+    def received(shape):
+        lead, (height, width) = shape[:-2], shape[-2:]
+        return [
+            [pltpu.VMEM(lead + (height // n, width), bf16) for n in (2, 4, 8)]
+            + [pltpu.VMEM(lead + (3, height // shards, width), bf16)]
+        ]
+
+    act, xgrad, *sums, small = pl.pallas_call(
         functools.partial(table_kernel, local, block_tables, seq),
         out_shape=(
             jax.ShapeDtypeStruct(block, bf16),
             jax.ShapeDtypeStruct(block, bf16),
-            jax.ShapeDtypeStruct(in_weight.shape, bf16),
+            jax.ShapeDtypeStruct(in_part, bf16),
             jax.ShapeDtypeStruct(out_weight.shape, bf16),
             jax.ShapeDtypeStruct(up_weight.shape, bf16),
             jax.ShapeDtypeStruct(down_weight.shape, bf16),
-            jax.ShapeDtypeStruct((LAYERS * 16, hidden), f32),
+            jax.ShapeDtypeStruct((LAYERS, 16, hidden), f32),
         ),
-        in_specs=[hbm, hbm] + [vmem] * 6,
-        out_specs=(hbm, hbm) + (vmem,) * 5,
+        in_specs=[hbm, hbm, vmem] + [hbm] * 4 + [vmem] * VECTORS,
+        out_specs=(hbm,) * 6 + (vmem,),
         scratch_shapes=[
+            pltpu.VMEM(in_weight.shape, bf16),
+            pltpu.VMEM(out_weight.shape, bf16),
+            pltpu.VMEM(up_weight.shape, bf16),
+            pltpu.VMEM(down_weight.shape, bf16),
+            pltpu.VMEM((LAYERS * VECTORS, hidden), f32),
+            pltpu.VMEM(in_part, bf16),
+            pltpu.VMEM(out_weight.shape, bf16),
+            pltpu.VMEM(up_weight.shape, bf16),
+            pltpu.VMEM(down_weight.shape, bf16),
+            pltpu.VMEM((LAYERS, 16, hidden), f32),
             pltpu.VMEM((LAYERS, rows, dim), bf16),
             pltpu.VMEM((rows, dim), bf16),
             pltpu.VMEM((rows, dim), f32),
@@ -836,21 +1206,34 @@
             pltpu.VMEM((1, seq), f32),
             pltpu.VMEM((seq, 1), f32),
             pltpu.VMEM((rows, 1), f32),
-            pltpu.VMEM((rows, dim), f32),
             pltpu.VMEM((rows, dim), bf16),
             pltpu.VMEM((rows, hidden), bf16),
             pltpu.VMEM((rows, dim), bf16),
             pltpu.VMEM((rows, dim), bf16),
             pltpu.VMEM((2 * HEADS, rows), f32),
             pltpu.VMEM((dim, rows), f32),
-            pltpu.VMEM((rows, 2 * dim), f32),
-            pltpu.VMEM((LAYERS, rows, 2 * dim), bf16),
-            pltpu.VMEM((LAYERS, rows, 2 * dim), bf16),
-            pltpu.VMEM((rows, 3 * dim), bf16),
+            pltpu.VMEM((rows, 2 * dim // groups), f32),
+            pltpu.VMEM((LAYERS, groups, rows, 2 * dim // groups), bf16),
+            pltpu.VMEM((LAYERS, groups, rows, 2 * dim // groups), bf16),
+            pltpu.VMEM((groups, rows, 3 * dim // groups), bf16),
             pltpu.VMEM((2, rows, dim), bf16),
         ]
+        + received(in_part)
+        + received(out_weight.shape)
+        + received(up_weight.shape)
+        + received(down_weight.shape)
+        + [
+            [pltpu.VMEM((LAYERS, 16, hidden // n), f32) for n in (2, 4, 8)]
+            + [pltpu.VMEM((LAYERS, 3, 16, hidden // 8), f32)]
+        ]
         + [dma((block_tables,))] * 8
-        + [dma((5,)), dma((LAYERS, 2)), dma((LAYERS, 2)), dma((2,))],
+        + [
+            dma((9,)),
+            dma((LAYERS, 2)),
+            dma((LAYERS, groups, 2)),
+            dma((2,)),
+            dma((LAYERS * 6, 2, 13)),
+        ],
         compiler_params=pltpu.CompilerParams(
             collective_id=0, has_side_effects=True, vmem_limit_bytes=62 * 1024 * 1024
         ),
@@ -862,41 +1245,83 @@
         out_weight,
         up_weight,
         down_weight,
-        vectors,
+        query_bias,
+        value_bias,
+        out_bias,
+        attn_gain,
+        attn_shift,
+        up_bias,
+        down_bias,
+        ffn_gain,
+        ffn_shift,
     )
-    count = jnp.sum(lengths.astype(f32)) / row_parts
-    totals = lax.psum((g_in, g_out, g_up, g_down, small, count), ("tables", "rows"))
-    g_in, g_out, g_up, g_down = [total.astype(f32) for total in totals[:4]]
-    small, count = totals[4:]
-    small = small.reshape(LAYERS, 16, hidden)
-    root_means = jnp.sqrt(jnp.sum(small[:, 10:13, :dim], axis=-1) / (count * dim))
-
-    def widen(values):
-        return jnp.swapaxes(values, 0, 1).astype(f32)
-
+    steps = 4
+
+    def whole(shape):
+        return pl.BlockSpec(shape, lambda l, i: (0,) * len(shape))
+
+    def sliced(height, width):
+        return pl.BlockSpec((1, height // steps, width), lambda l, i: (l, i, 0))
+
+    weights = [
+        sliced(dim, 3 * dim),
+        sliced(dim, dim),
+        sliced(dim, hidden),
+        sliced(hidden, dim),
+    ]
+    cut = local // (LAYERS * steps)
+    table_rows = pl.BlockSpec((block_tables, cut, dim), lambda l, i: (0, l * steps + i, 0))
+    row_tables = pl.BlockSpec((cut, block_tables, dim), lambda l, i: (l * steps + i, 0, 0))
+    vector = jax.ShapeDtypeStruct((LAYERS, dim), f32)
+    wide_vector = jax.ShapeDtypeStruct((LAYERS, hidden), f32)
+    shapes = [
+        jax.ShapeDtypeStruct(tables_in.shape, f32),
+        jax.ShapeDtypeStruct(tables_in.shape, f32),
+        jax.ShapeDtypeStruct(in_weight.shape, f32),
+        jax.ShapeDtypeStruct(out_weight.shape, f32),
+        jax.ShapeDtypeStruct(up_weight.shape, f32),
+        jax.ShapeDtypeStruct(down_weight.shape, f32),
+        jax.ShapeDtypeStruct((LAYERS, 3), f32),
+    ] + [vector] * 5 + [wide_vector] + [vector] * 3
+    outs = pl.pallas_call(
+        widen_kernel,
+        grid=(LAYERS, steps),
+        out_shape=shapes,
+        in_specs=[
+            pl.BlockSpec((1, groups, dim // steps, 3 * dim // groups), lambda l, i: (l, 0, i, 0)),
+            *weights[1:],
+            table_rows,
+            table_rows,
+            whole((LAYERS, 16, hidden)),
+        ],
+        out_specs=[row_tables, row_tables, *weights] + [whole(s.shape) for s in shapes[6:]],
+        compiler_params=pltpu.CompilerParams(vmem_limit_bytes=48 * 1024 * 1024),
+    )(*sums, act, xgrad, small)
+    act, xgrad, g_in, g_out, g_up, g_down, root_means = outs[:7]
+    query, value, out, gain1, shift1, up, down, gain2, shift2 = outs[7:]
     return (
-        widen(act),
-        widen(xgrad),
+        act,
+        xgrad,
         g_in,
-        small[:, 0, :dim],
-        small[:, 1, :dim],
+        query,
+        value,
         g_out,
-        small[:, 3, :dim],
-        small[:, 4, :dim],
-        small[:, 5, :dim],
+        out,
+        gain1,
+        shift1,
         g_up,
-        small[:, 6],
+        up,
         g_down,
-        small[:, 7, :dim],
-        small[:, 8, :dim],
-        small[:, 9, :dim],
+        down,
+        gain2,
+        shift2,
         root_means,
     )
 
 
 def per_device(tables, row_parts, *operands):
     local, block_tables, dim = operands[0].shape
-    if tables % 2 == 0 and row_parts == 2 * block_tables and local * row_parts <= 1024:
+    if tables == 4 and row_parts == 2 * block_tables and local * row_parts <= 1024:
         return table_device(tables, row_parts, *operands)
     return gathered_device(*operands)
 

time: 451 us -> 205 us (0.45)
  waiting for transfers between devices: 258 us -> 0 us
  Pallas kernels: 91.6 us -> 193 us
  blocking collectives: 51.5 us -> 0 us
  between operations: 15.4 us -> 0.83 us
  other arithmetic: 14.1 us -> 0.75 us
  local copies, waits for them, and re-layouts: 19.7 us -> 8.82 us
    psum x2 -> x0, waiting for transfers between devices: 257 us -> none  [table_device(): lax.psum((g_in, g_out, g_up, g_down, small, count), ('tables', 'rows'))]
    pallas_call x1, Pallas kernels: 91.6 us -> 183 us  [table_device(): pl.pallas_call(functools.partial(table_kernel, local, block_tables, seq),...]
    psum x1 -> x0, blocking collectives: 51.5 us -> none  [table_device(): lax.psum((g_in, g_out, g_up, g_down, small, count), ('tables', 'rows'))]
    convert_element_type x5 -> x0, other arithmetic: 12.6 us -> none  [the longest x4 12.3 us: table_device(): g_in, g_out, g_up, g_down = [total.astype(f32) for total in totals[:4]]]
    pallas_call x0 -> x1, Pallas kernels: none -> 10.1 us  [table_device(): pl.pallas_call(widen_kernel, grid=(LAYERS, steps), out_shape=shapes, in_s...]
    unnamed x27 -> x10, local copies, waits for them, and re-layouts: 13.4 us -> 5.79 us
  transfers between devices with their start and end apart: 2 -> 0, of which waited for: 2 -> 0; matrix products, arithmetic and copies ran while one was open for 2% -> 0% of each run, Pallas kernels for 0% -> 0%
where the time goes in v2:
time: 205 us; the launch traced here: 203 us
  Pallas kernels  193 us (94%)
  local copies, waits for them, and re-layouts  8.82 us (4%)
    pallas_call x1, Pallas kernels, table_device(): pl.pallas_call(functools.partial(table_kernel, local, block_tables, seq),...  183 us
    pallas_call x1, Pallas kernels, table_device(): pl.pallas_call(widen_kernel, grid=(LAYERS, steps), out_shape=shapes, in_s...  10.1 us
    unnamed x10, local copies, waits for them, and re-layouts  5.79 us

profile of v2, /device:TPU:0, one launch (start us, length us, event | category | flops | bytes accessed | tf_op | source)
XLA Modules:
  0.0 203.1 jit_solution(18078622199806389576)
XLA Ops:
  0.6 0.7 pad_add_fusion
  1.4 0.7 broadcast_in_dim.2.meta_ref
  2.1 2.4 %copy_bitcast_fusion = (bf16[4,128,512]{2,1,0:T(8,128)(2,1)}, bf16[4,128,512]{2,1,0:T(8,128)(2,1)}) fusion(bf16[128,4,512]{2,1,0:T(4,128)(2,1)} %param.31, bf16[128,4,512]{2,1,0:T(4,128)(2,1)} %param.17), kind=kLoop, calls=%fused_computation | loop fusion | bytes 2097152 | tf_op jit(solution)/shard_map/transpose | solution.py:1242
  4.4 182.7 %shard_map.288 = (bf16[4,128,512]{2,1,0:T(8,128)(2,1)}, bf16[4,128,512]{2,1,0:T(8,128)(2,1)}, bf16[2,2,512,768]{3,2,1,0:T(8,128)(2,1)}, bf16[2,512,512]{2,1,0:T(...) custom-call(bf16[4,128,512]{2,1,0:T(8,128)(2,1)} %get-tuple-element.63.x_hbm, ...), custom_call_target="tpu_custom_call" | custom-call | tf_op jit(solution)/shard_map/pallas_call | solution.py:1167
  187.1 0.0 copy-start
  187.1 1.6 copy-done
  188.7 0.0 copy-start.1
  188.7 1.2 copy-done.1
  189.9 0.0 copy-start.2
  189.9 1.0 copy-done.2
  191.0 0.0 copy-start.3
  191.0 1.0 copy-done.3
  192.0 0.0 copy-start.4
  192.0 0.9 copy-done.4
  192.9 10.1 %shard_map.289 = (f32[128,4,512]{2,1,0:T(4,128)}, f32[128,4,512]{2,1,0:T(4,128)}, f32[2,512,1536]{2,1,0:T(8,128)}, f32[2,512,512]{2,1,0:T(8,128)}, f32[2,512,102...) custom-call(bf16[2,2,512,768]{3,2,1,0:T(8,128)(2,1)} %get-tuple-elem, ...), custom_call_target="tpu_custom_call" | custom-call | tf_op jit(solution)/shard_map/pallas_call | solution.py:1286
Async XLA Ops:
  187.1 1.6 copy-start
  188.7 1.2 copy-start.1
  189.9 1.0 copy-start.2
  191.0 1.0 copy-start.3
  192.0 0.9 copy-start.4

commit v3 on v2

--- a/solution.py
+++ b/solution.py
@@ -341,7 +341,52 @@
 TN = (((0,), (0,)), ((), ()))
 TILE = 256
 VECTORS = 9
-GROUPS = 2
+GROUPS = 4
+HALVES = 2
+SCHEDULE = (
+    (),
+    (),
+    (0, 1),
+    (),
+    (),
+    (),
+    (),
+    (2, 0, 1, 3, 4),
+    (),
+    (),
+    (5,),
+    (),
+    (0, 1),
+    (2, 6),
+    (3, 4, 5),
+    (),
+    (2, 7, 0, 1),
+    (3, 4, 5, 6, 8, 7, 9),
+    (),
+    (2, 0, 6, 1, 7, 9, 8, 10, 11),
+    (3, 4, 5),
+    (9,),
+    (0,),
+    (1, 2, 6, 7, 8),
+    (10, 11, 12, 13, 14, 9),
+    (0,),
+    (2, 5),
+    (0, 3, 4),
+    (1, 6, 7, 8, 9, 10, 11, 15),
+    (),
+    (1,),
+    (5, 16),
+    (9,),
+    (8, 12, 10, 11, 13, 3, 4, 6, 7, 14, 17),
+    (),
+    (2, 9, 15, 18, 19),
+    (
+        10, 11, 9, 2, 8, 5, 16, 5, 12, 13, 14, 19, 15, 6, 7, 12, 17, 10, 11, 16, 19, 13, 3, 4, 6, 7,
+        18, 8, 14, 15, 17, 3, 19, 4, 8, 18, 10, 11, 12, 16, 19, 10, 11, 12, 13, 15, 19, 14, 17, 18,
+        16, 13, 19, 15, 17, 14, 12, 19, 16, 18, 12, 13, 17, 13, 15, 18, 16, 14, 15, 17, 16, 14, 18,
+        17, 18,
+    ),
+)
 
 
 def dot(left, right, dims=NN):
@@ -367,8 +412,8 @@
             pltpu.make_async_remote_copy(
                 src_ref=part.at[pl.ds(give, size)],
                 dst_ref=recv[n],
-                send_sem=sems.at[0, n],
-                recv_sem=sems.at[1, n],
+                send_sem=sems.at[0],
+                recv_sem=sems.at[3 + n],
                 device_id=partner,
                 device_id_type=MESH,
             )
@@ -379,8 +424,8 @@
             pltpu.make_async_remote_copy(
                 src_ref=total.at[pl.ds(keep, size)],
                 dst_ref=total.at[pl.ds(keep, size)],
-                send_sem=sems.at[0, 3 + n],
-                recv_sem=sems.at[1, 3 + n],
+                send_sem=sems.at[0],
+                recv_sem=sems.at[9 + n],
                 device_id=partner,
                 device_id_type=MESH,
             )
@@ -398,8 +443,8 @@
             pltpu.make_async_remote_copy(
                 src_ref=part.at[piece(index)],
                 dst_ref=recv[3].at[n],
-                send_sem=sems.at[0, 6 + n],
-                recv_sem=sems.at[1, 6 + n],
+                send_sem=sems.at[n],
+                recv_sem=sems.at[6 + n],
                 device_id=peer,
                 device_id_type=MESH,
             )
@@ -408,13 +453,13 @@
             pltpu.make_async_remote_copy(
                 src_ref=part.at[mine],
                 dst_ref=total.at[mine],
-                send_sem=sems.at[0, 9 + n],
-                recv_sem=sems.at[1, 9 + n],
+                send_sem=sems.at[n],
+                recv_sem=sems.at[12 + n],
                 device_id=peer,
                 device_id_type=MESH,
             )
         )
-    kept = pltpu.make_async_copy(part.at[mine], total.at[mine], sems.at[0, 12])
+    kept = pltpu.make_async_copy(part.at[mine], total.at[mine], sems.at[15])
 
     def add(n):
         size = sizes[n + 1]
@@ -481,8 +526,8 @@
             pltpu.make_async_remote_copy(
                 src_ref=part.at[:, give],
                 dst_ref=recv[n],
-                send_sem=sems.at[0, n],
-                recv_sem=sems.at[1, n],
+                send_sem=sems.at[0],
+                recv_sem=sems.at[3 + n],
                 device_id=partner,
                 device_id_type=MESH,
             )
@@ -491,8 +536,8 @@
             pltpu.make_async_remote_copy(
                 src_ref=total.at[:, keep],
                 dst_ref=total.at[:, keep],
-                send_sem=sems.at[0, 3 + n],
-                recv_sem=sems.at[1, 3 + n],
+                send_sem=sems.at[0],
+                recv_sem=sems.at[9 + n],
                 device_id=partner,
                 device_id_type=MESH,
             )
@@ -504,8 +549,8 @@
         pltpu.make_async_remote_copy(
             src_ref=part.at[:, mine],
             dst_ref=recv[3].at[n],
-            send_sem=sems.at[0, 6 + n],
-            recv_sem=sems.at[1, 6 + n],
+            send_sem=sems.at[n],
+            recv_sem=sems.at[6 + n],
             device_id=peer,
             device_id_type=MESH,
         )
@@ -550,7 +595,8 @@
     seq,
     x_hbm,
     cot_hbm,
-    meta_ref,
+    lengths_ref,
+    counts_ref,
     w_in_hbm,
     w_out_hbm,
     w_up_hbm,
@@ -754,26 +800,24 @@
 
     x_start()
     loads = [
-        pltpu.make_async_copy(source, target, local_sem.at[5 + n])
+        pltpu.make_async_copy(source, target, local_sem.at[4 + n])
         for n, (source, target) in enumerate(
             ((w_in_hbm, w_in), (w_out_hbm, w_out), (w_up_hbm, w_up), (w_down_hbm, w_down))
         )
     ]
     for load in loads:
         load.start()
-    cot_start()
     for n, ref in enumerate(vector_refs):
         for layer in range(LAYERS):
             vectors[pl.ds(layer * VECTORS + n, 1), pl.ds(0, ref.shape[1])] = ref[...].astype(
                 jnp.float32
             )[layer : layer + 1, :]
-    meta_own = pltpu.make_async_copy(meta_ref, meta.at[core], local_sem.at[4])
-    meta_own.start()
-    meta_copy = swap(meta_ref, meta.at[core], meta_sem)
+    for k in range(block_tables):
+        meta[core, pl.ds(k, 1), :] = jnp.full((1, 128), lengths_ref[k], jnp.int32)
+        meta[core, pl.ds(block_tables + k, 1), :] = jnp.full((1, 128), counts_ref[k], jnp.int32)
+    meta_copy = swap(meta.at[core], meta.at[core], meta_sem)
     meta_copy.start()
-
     small[...] = jnp.zeros_like(small)
-    meta_own.wait()
     meta_copy.wait()
     length = meta[side, pl.ds(slot, 1), :][:, :1]
     train = meta[side, pl.ds(slot + block_tables, 1), :][:, :1]
@@ -784,6 +828,7 @@
     )
     small[0, pl.ds(13, 1), pl.ds(0, 128)] = jnp.broadcast_to(column_sum(valid[...]), (1, 128))
     x_arrive()
+    cot_start()
     loads[0].wait()
 
     def vector(index, layer, width):
@@ -793,9 +838,15 @@
         at = (layer, pl.ds(index, 1), pl.ds(0, values.shape[-1]))
         small[at] = small[at] + values
 
-    def each_tile(body):
+    def each_tile(body, after=()):
         def step(i, carry):
             body(pl.ds(pl.multiple_of(i * TILE, TILE), TILE))
+            for n, run in enumerate(after):
+
+                @pl.when(i == n)
+                def _():
+                    run()
+
             return carry
 
         lax.fori_loop(0, tiles, step, 0)
@@ -810,23 +861,33 @@
                 (projected[:, :dim] + vector(0, layer, dim)) * scale
             ).astype(jnp.bfloat16)
             own = pl.ds(pl.multiple_of(own_rows + at.start, TILE), TILE)
-            kv[layer, own, pl.ds(0, dim)] = projected[:, dim : 2 * dim].astype(jnp.bfloat16)
-            kv[layer, own, pl.ds(dim, dim)] = (
-                projected[:, 2 * dim :] + vector(1, layer, dim)
-            ).astype(jnp.bfloat16)
+            key_rows = projected[:, dim : 2 * dim].astype(jnp.bfloat16)
+            value_rows = (projected[:, 2 * dim :] + vector(1, layer, dim)).astype(jnp.bfloat16)
+            for h in range(HEADS):
+                cols = slice(h * head_dim, (h + 1) * head_dim)
+                kv[layer, h, own, pl.ds(0, head_dim)] = key_rows[:, cols]
+                kv[layer, h, own, pl.ds(head_dim, head_dim)] = value_rows[:, cols]
 
         each_tile(project)
-        mine = kv.at[layer, pl.ds(own_rows, rows)]
-        kv_copy = swap(mine, mine, kv_sem.at[layer])
-        kv_copy.start()
-        kv_copy.wait()
+
+        def kv_copy(h):
+            mine = kv.at[layer, h, pl.ds(own_rows, rows)]
+            return swap(mine, mine, kv_sem.at[layer, h])
+
+        for h in range(HEADS):
+            kv_copy(h).start()
 
         def attend(step, carry):
             h = step // tiles
             at = pl.ds(pl.multiple_of(lax.rem(step, tiles) * TILE, TILE), TILE)
             cols = head_cols(h)
-            key_rows = kv[layer, :, cols]
-            value_rows = kv[layer, :, pl.ds(pl.multiple_of(dim + h * head_dim, head_dim), head_dim)]
+
+            @pl.when(lax.rem(step, tiles) == 0)
+            def _():
+                kv_copy(h).wait()
+
+            key_rows = kv[layer, h, :, pl.ds(0, head_dim)]
+            value_rows = kv[layer, h, :, pl.ds(head_dim, head_dim)]
             scores = dot(queries[layer, at, cols], key_rows, NT) + bias_row[...]
             row_max = jnp.max(scores, axis=-1, keepdims=True)
             exponent = jnp.exp(scores - row_max)
@@ -889,21 +950,31 @@
 
     jobs = []
 
+    points = list(SCHEDULE)
+
     def begin(steps):
         jobs.append(list(steps))
         jobs[-1].pop(0)()
 
     def tick():
-        for steps in jobs:
-            if steps:
-                steps.pop(0)()
-
-    def job(index, part, total, recv):
-        return reduce_job(part, total, recv, job_sem.at[index], halves, z_peers, z_side)
+        for index in points.pop(0):
+            if index < len(jobs) and jobs[index]:
+                jobs[index].pop(0)()
+
+    def reduce(part, total, recv):
+        begin(reduce_job(part, total, recv, job_sem.at[len(jobs)], halves, z_peers, z_side))
+
+    def reduce_halves(part, total, recv):
+        width = part.shape[1] // HALVES
+        for n in range(HALVES):
+            cols = pl.ds(n * width, width)
+            reduce(
+                part.at[:, cols],
+                total.at[:, cols],
+                [ref.at[:, cols] for ref in recv[:3]] + [recv[3].at[:, :, cols]],
+            )
 
     def backward(layer):
-        first_job = (LAYERS - 1 - layer) * 6
-
         def recv_of(refs):
             return [ref.at[layer] for ref in refs]
 
@@ -927,7 +998,7 @@
         each_tile(enter)
         g_down[layer] = dot(act_low[layer], ffn_low[...], TN).astype(jnp.bfloat16)
         tick()
-        begin(job(first_job, g_down.at[layer], t_down.at[layer], recv_of(recv_down)))
+        reduce_halves(g_down.at[layer], t_down.at[layer], recv_of(recv_down))
 
         def dense(at):
             hidden = (dot(ffn_low[at, :], w_down[layer], NT) * slope[layer, at, :]).astype(
@@ -957,13 +1028,13 @@
                 held = jnp.where(lane == HEADS + h, center, held)
             stats_rows[:, at] = jnp.transpose(held)[: 2 * HEADS, :]
 
-        each_tile(dense)
+        each_tile(dense, (tick,) * tiles)
+        g_up[layer] = dot(mid_low[layer], hidden_low[...], TN).astype(jnp.bfloat16)
         tick()
-        g_up[layer] = dot(mid_low[layer], hidden_low[...], TN).astype(jnp.bfloat16)
-        begin(job(first_job + 1, g_up.at[layer], t_up.at[layer], recv_of(recv_up)))
+        reduce_halves(g_up.at[layer], t_up.at[layer], recv_of(recv_up))
         g_out[layer] = dot(attended[layer], branch_low[...], TN).astype(jnp.bfloat16)
         tick()
-        begin(job(first_job + 2, g_out.at[layer], t_out.at[layer], recv_of(recv_out)))
+        reduce(g_out.at[layer], t_out.at[layer], recv_of(recv_out))
 
         def attend(group, base, first, keep):
             def step(i, carry):
@@ -971,15 +1042,14 @@
                 j = pl.multiple_of(lax.rem(i, tiles) * TILE, TILE)
                 at = pl.ds(pl.multiple_of(base + j, TILE), TILE)
                 cols = head_cols(h)
-                value_cols = pl.ds(pl.multiple_of(dim + h * head_dim, head_dim), head_dim)
-                key_rows = kv[layer, at, cols]
+                key_rows = kv[layer, h, at, pl.ds(0, head_dim)]
                 query_rows = queries[layer, :, cols]
                 grads = attended_low[:, cols]
                 probs = jnp.exp(
                     dot(key_rows, query_rows, NT) + bias_col[at, :] - stats_rows[pl.ds(h, 1), :]
                 )
                 value_part = dot(probs.astype(jnp.bfloat16), grads)
-                probs_grad = dot(kv[layer, at, value_cols], grads, NT)
+                probs_grad = dot(kv[layer, h, at, pl.ds(head_dim, head_dim)], grads, NT)
                 scores_low = (probs * (probs_grad - stats_rows[pl.ds(HEADS + h, 1), :])).astype(
                     jnp.bfloat16
                 )
@@ -1001,30 +1071,35 @@
 
             lax.fori_loop(0, group_heads * tiles, step, 0)
 
-        for group in range(GROUPS):
-
-            def keep_sent(at, cols, part):
+        def dkv_copy(group):
+            return swap(
+                dkv_send.at[layer, group], dkv_recv.at[layer, group], dkv_sem.at[layer, group]
+            )
+
+        def attend_peer(group):
+            def keep(at, cols, part):
                 dkv_send[layer, group, at, cols] = part.astype(jnp.bfloat16)
 
-            def keep_own(at, cols, part):
-                dkv_own[at, cols] = part
-
-            attend(group, peer_rows, True, keep_sent)
-            copy = swap(
-                dkv_send.at[layer, group], dkv_recv.at[layer, group], dkv_sem.at[layer, group]
-            )
-            copy.start()
+            attend(group, peer_rows, True, keep)
+            dkv_copy(group).start()
             tick()
-            attend(group, own_rows, False, keep_own)
+
+        def attend_own(group):
+            def keep(at, cols, part):
+                dkv_own[group % 2, at, cols] = part
+
+            attend(group, own_rows, False, keep)
             tick()
-            copy.wait()
+
+        def finish_group(group):
+            dkv_copy(group).wait()
 
             def finish(at):
                 group_rows = pl.ds(group * group_width, group_width)
                 query = jnp.transpose(dq_t[group_rows, at]).astype(jnp.bfloat16)
-                pair = (dkv_own[at, :] + dkv_recv[layer, group, at, :].astype(jnp.float32)).astype(
-                    jnp.bfloat16
-                )
+                pair = (
+                    dkv_own[group % 2, at, :] + dkv_recv[layer, group, at, :].astype(jnp.float32)
+                ).astype(jnp.bfloat16)
                 proj_low[group, at, pl.ds(0, group_width)] = query
                 proj_low[group, at, pl.ds(group_width, 2 * group_width)] = pair
                 cols = pl.ds(group * group_width, group_width)
@@ -1041,20 +1116,25 @@
             g_in[layer, group, :, pl.ds(group_width, 2 * group_width)] = grad[
                 :, group_width:
             ].astype(jnp.bfloat16)
-            begin(
-                job(
-                    first_job + 3 + group,
-                    g_in.at[layer, group],
-                    t_in.at[layer, group],
-                    [ref.at[layer, group] for ref in recv_in],
-                )
-            )
+            tick()
+            reduce(
+                g_in.at[layer, group],
+                t_in.at[layer, group],
+                [ref.at[layer, group] for ref in recv_in],
+            )
+
+        for group in range(GROUPS):
+            attend_peer(group)
+            if group > 0:
+                finish_group(group - 1)
+            attend_own(group)
+        finish_group(GROUPS - 1)
         begin(
             small_job(
                 small.at[layer],
                 t_small.at[layer],
                 [ref.at[layer] for ref in recv_small],
-                job_sem.at[first_job + 5],
+                job_sem.at[len(jobs)],
                 halves,
                 z_peers,
             )
@@ -1076,14 +1156,17 @@
                 staged[1, at, :] = grad.astype(jnp.bfloat16)
 
         each_tile(pass_down)
+        tick()
         if layer == 0:
             xg_start()
-        tick()
 
     for layer in reversed(range(LAYERS)):
         backward(layer)
+    tick()
     while any(jobs):
-        tick()
+        for steps in jobs:
+            if steps:
+                steps.pop(0)()
     act_arrive()
     xg_arrive()
     x_left()
@@ -1149,9 +1232,9 @@
     head_dim = dim // HEADS
     f32, bf16 = jnp.float32, jnp.bfloat16
     groups = GROUPS
-    meta = jnp.broadcast_to(jnp.concatenate([lengths, train_counts])[:, None], (2 * block_tables, 128))
     vmem = pl.BlockSpec(memory_space=pltpu.VMEM)
     hbm = pl.BlockSpec(memory_space=pl.ANY)
+    smem = pl.BlockSpec(memory_space=pltpu.SMEM)
     block = (block_tables, local, dim)
     dma = pltpu.SemaphoreType.DMA
     in_part = (LAYERS, groups, dim, 3 * dim // groups)
@@ -1175,7 +1258,7 @@
             jax.ShapeDtypeStruct(down_weight.shape, bf16),
             jax.ShapeDtypeStruct((LAYERS, 16, hidden), f32),
         ),
-        in_specs=[hbm, hbm, vmem] + [hbm] * 4 + [vmem] * VECTORS,
+        in_specs=[hbm, hbm, smem, smem] + [hbm] * 4 + [vmem] * VECTORS,
         out_specs=(hbm,) * 6 + (vmem,),
         scratch_shapes=[
             pltpu.VMEM(in_weight.shape, bf16),
@@ -1192,7 +1275,7 @@
             pltpu.VMEM((rows, dim), bf16),
             pltpu.VMEM((rows, dim), f32),
             pltpu.VMEM((LAYERS, rows, dim), bf16),
-            pltpu.VMEM((LAYERS, seq, 2 * dim), bf16),
+            pltpu.VMEM((LAYERS, HEADS, seq, 2 * head_dim), bf16),
             pltpu.VMEM((LAYERS, rows, dim), bf16),
             pltpu.VMEM((LAYERS, rows, head_dim), f32),
             pltpu.VMEM((LAYERS, rows, dim), f32),
@@ -1212,7 +1295,7 @@
             pltpu.VMEM((rows, dim), bf16),
             pltpu.VMEM((2 * HEADS, rows), f32),
             pltpu.VMEM((dim, rows), f32),
-            pltpu.VMEM((rows, 2 * dim // groups), f32),
+            pltpu.VMEM((2, rows, 2 * dim // groups), f32),
             pltpu.VMEM((LAYERS, groups, rows, 2 * dim // groups), bf16),
             pltpu.VMEM((LAYERS, groups, rows, 2 * dim // groups), bf16),
             pltpu.VMEM((groups, rows, 3 * dim // groups), bf16),
@@ -1228,11 +1311,11 @@
         ]
         + [dma((block_tables,))] * 8
         + [
-            dma((9,)),
-            dma((LAYERS, 2)),
+            dma((8,)),
+            dma((LAYERS, HEADS, 2)),
             dma((LAYERS, groups, 2)),
             dma((2,)),
-            dma((LAYERS * 6, 2, 13)),
+            dma((LAYERS * (2 * HALVES + 2 + groups), 16)),
         ],
         compiler_params=pltpu.CompilerParams(
             collective_id=0, has_side_effects=True, vmem_limit_bytes=62 * 1024 * 1024
@@ -1240,7 +1323,8 @@
     )(
         jnp.swapaxes(tables_in, 0, 1),
         jnp.swapaxes(cotangent, 0, 1),
-        meta,
+        lengths,
+        train_counts,
         in_weight,
         out_weight,
         up_weight,
@@ -1295,7 +1379,7 @@
             whole((LAYERS, 16, hidden)),
         ],
         out_specs=[row_tables, row_tables, *weights] + [whole(s.shape) for s in shapes[6:]],
-        compiler_params=pltpu.CompilerParams(vmem_limit_bytes=48 * 1024 * 1024),
+        compiler_params=pltpu.CompilerParams(vmem_limit_bytes=62 * 1024 * 1024),
     )(*sums, act, xgrad, small)
     act, xgrad, g_in, g_out, g_up, g_down, root_means = outs[:7]
     query, value, out, gain1, shift1, up, down, gain2, shift2 = outs[7:]

time: 205 us -> 167 us (0.81)
  Pallas kernels: 193 us -> 163 us
  local copies, waits for them, and re-layouts: 8.82 us -> 2.37 us
    pallas_call x1, Pallas kernels: 183 us -> 152 us  [table_device(): pl.pallas_call(functools.partial(table_kernel, local, block_tables, seq),...]
    unnamed x10 -> x0, local copies, waits for them, and re-layouts: 5.79 us -> none
where the time goes in v3:
time: 167 us; the launch traced here: 166 us
  Pallas kernels  163 us (98%)
  local copies, waits for them, and re-layouts  2.37 us (1%)
    pallas_call x1, Pallas kernels, table_device(): pl.pallas_call(functools.partial(table_kernel, local, block_tables, seq),...  152 us
    pallas_call x1, Pallas kernels, table_device(): pl.pallas_call(widen_kernel, grid=(LAYERS, steps), out_shape=shapes, in_s...  11.6 us

profile of v3, /device:TPU:0, one launch (start us, length us, event | category | flops | bytes accessed | tf_op | source)
XLA Modules:
  0.0 166.5 jit_solution(11408431336568169797)
XLA Ops:
  0.6 2.4 %copy_bitcast_fusion = (bf16[4,128,512]{2,1,0:T(8,128)(2,1)}, bf16[4,128,512]{2,1,0:T(8,128)(2,1)}) fusion(bf16[128,4,512]{2,1,0:T(4,128)(2,1)} %param.31, bf16[128,4,512]{2,1,0:T(4,128)(2,1)} %param.17), kind=kLoop, calls=%fused_computation | loop fusion | bytes 2097152 | tf_op jit(solution)/shard_map/transpose | solution.py:1325
  3.0 151.7 %shard_map.288 = (bf16[4,128,512]{2,1,0:T(8,128)(2,1)}, bf16[4,128,512]{2,1,0:T(8,128)(2,1)}, bf16[2,4,512,384]{3,2,1,0:T(8,128)(2,1)}, bf16[2,512,512]{2,1,0:T(...) custom-call(bf16[4,128,512]{2,1,0:T(8,128)(2,1)} %get-tuple-element.63.x_hbm, ...), custom_call_target="tpu_custom_call" | custom-call | tf_op jit(solution)/shard_map/pallas_call | solution.py:1250
  154.8 11.6 %shard_map.289 = (f32[128,4,512]{2,1,0:T(4,128)}, f32[128,4,512]{2,1,0:T(4,128)}, f32[2,512,1536]{2,1,0:T(8,128)}, f32[2,512,512]{2,1,0:T(8,128)}, f32[2,512,102...) custom-call(bf16[2,4,512,384]{3,2,1,0:T(8,128)(2,1)} %get-tuple-elem, ...), custom_call_target="tpu_custom_call" | custom-call | tf_op jit(solution)/shard_map/pallas_call | solution.py:1370

commit v4 on v3

--- a/solution.py
+++ b/solution.py
@@ -343,6 +343,13 @@
 VECTORS = 9
 GROUPS = 4
 HALVES = 2
+PATHS = {
+    "A": ("cxy", "cyx"),
+    "N": ("cnyxf", "cnyxf"),
+    "P": ("cxynf", "cxynf"),
+    "Q": ("cyxnf", "cyxnf"),
+}
+KINDS = "NAAAQNAANAQPANANAAAA"
 SCHEDULE = (
     (),
     (),
@@ -351,40 +358,40 @@
     (),
     (),
     (),
-    (2, 0, 1, 3, 4),
+    (),
+    (2, 1, 3, 4),
+    (),
+    (0, 5),
     (),
     (),
-    (5,),
     (),
-    (0, 1),
-    (2, 6),
-    (3, 4, 5),
+    (1, 6),
     (),
-    (2, 7, 0, 1),
-    (3, 4, 5, 6, 8, 7, 9),
+    (5, 7),
+    (0, 1, 2, 3, 4, 8, 9),
+    (5, 6),
+    (0, 1, 7),
+    (8, 9, 10, 11, 2, 5, 3, 4),
+    (0, 6),
+    (1, 7),
+    (9,),
     (),
-    (2, 0, 6, 1, 7, 9, 8, 10, 11),
-    (3, 4, 5),
-    (9,),
-    (0,),
-    (1, 2, 6, 7, 8),
-    (10, 11, 12, 13, 14, 9),
-    (0,),
-    (2, 5),
-    (0, 3, 4),
-    (1, 6, 7, 8, 9, 10, 11, 15),
+    (8, 5, 12, 13, 14),
+    (11, 4, 10),
+    (1,),
+    (0, 8, 9, 15, 2),
+    (1, 3, 5, 6, 7, 4),
+    (12, 11, 13),
+    (0, 8, 9, 10, 14, 5, 16),
     (),
-    (1,),
-    (5, 16),
-    (9,),
-    (8, 12, 10, 11, 13, 3, 4, 6, 7, 14, 17),
     (),
-    (2, 9, 15, 18, 19),
+    (12, 17),
+    (2, 4, 6, 7, 8, 9, 11, 3, 13, 10, 18, 19),
     (
-        10, 11, 9, 2, 8, 5, 16, 5, 12, 13, 14, 19, 15, 6, 7, 12, 17, 10, 11, 16, 19, 13, 3, 4, 6, 7,
-        18, 8, 14, 15, 17, 3, 19, 4, 8, 18, 10, 11, 12, 16, 19, 10, 11, 12, 13, 15, 19, 14, 17, 18,
-        16, 13, 19, 15, 17, 14, 12, 19, 16, 18, 12, 13, 17, 13, 15, 18, 16, 14, 15, 17, 16, 14, 18,
-        17, 18,
+        5, 15, 0, 14, 12, 16, 4, 11, 10, 8, 17, 9, 13, 2, 6, 19, 7, 9, 15, 3, 11, 16, 10, 14, 8, 12,
+        13, 4, 19, 5, 17, 18, 15, 5, 11, 13, 19, 6, 12, 7, 0, 10, 15, 18, 16, 2, 4, 3, 14, 17, 6,
+        19, 7, 13, 11, 8, 0, 15, 2, 4, 3, 8, 10, 19, 18, 16, 13, 17, 14, 15, 12, 19, 18, 12, 19, 16,
+        17, 11, 15, 13, 10, 18, 11, 14, 13, 10, 16, 17, 14, 15, 18, 16, 17, 15, 18,
     ),
 )
 
@@ -403,7 +410,9 @@
 
 def reduce_job(part, total, recv, sems, halves, z_peers, quarter):
     rows = part.shape[0]
+    shard = recv[3].shape[0] // 3
     offsets, sizes, copies, back = [0], [rows], [], []
+    targets = recv[:3] + [recv[3].at[pl.ds(0, 2 * shard)], recv[3].at[pl.ds(2 * shard, shard)]]
     for n, (partner, bit) in enumerate(halves):
         size = sizes[-1] // 2
         keep = pl.multiple_of(offsets[-1] + bit * size, size)
@@ -411,40 +420,41 @@
         copies.append(
             pltpu.make_async_remote_copy(
                 src_ref=part.at[pl.ds(give, size)],
-                dst_ref=recv[n],
+                dst_ref=targets[n],
                 send_sem=sems.at[0],
-                recv_sem=sems.at[3 + n],
+                recv_sem=sems.at[1 + n],
                 device_id=partner,
                 device_id_type=MESH,
             )
         )
         offsets.append(keep)
         sizes.append(size)
+        held = part if size == shard else total
         back.append(
             pltpu.make_async_remote_copy(
-                src_ref=total.at[pl.ds(keep, size)],
+                src_ref=held.at[pl.ds(keep, size)],
                 dst_ref=total.at[pl.ds(keep, size)],
                 send_sem=sems.at[0],
-                recv_sem=sems.at[9 + n],
+                recv_sem=sems.at[6 + n],
                 device_id=partner,
                 device_id_type=MESH,
             )
         )
-    size = sizes[-1] // (len(z_peers) + 1)
+    last = len(halves) - 1
     base = offsets[-1]
 
     def piece(index):
-        return pl.ds(pl.multiple_of(base + index * size, size), size)
-
-    mine = piece(quarter)
+        return pl.ds(pl.multiple_of(base + index * shard, shard), shard)
+
+    mine = piece(quarter if z_peers else 0)
     spread, gather = [], []
     for n, (peer, index) in enumerate(z_peers):
         spread.append(
             pltpu.make_async_remote_copy(
                 src_ref=part.at[piece(index)],
-                dst_ref=recv[3].at[n],
-                send_sem=sems.at[n],
-                recv_sem=sems.at[6 + n],
+                dst_ref=recv[3].at[pl.ds(n * shard, shard)],
+                send_sem=sems.at[0],
+                recv_sem=sems.at[4],
                 device_id=peer,
                 device_id_type=MESH,
             )
@@ -453,13 +463,23 @@
             pltpu.make_async_remote_copy(
                 src_ref=part.at[mine],
                 dst_ref=total.at[mine],
-                send_sem=sems.at[n],
-                recv_sem=sems.at[12 + n],
+                send_sem=sems.at[0],
+                recv_sem=sems.at[9],
                 device_id=peer,
                 device_id_type=MESH,
             )
         )
-    kept = pltpu.make_async_copy(part.at[mine], total.at[mine], sems.at[15])
+    kept = pltpu.make_async_copy(part.at[mine], total.at[mine], sems.at[11])
+
+    def wait_all(recv_sem):
+        pltpu.make_async_remote_copy(
+            src_ref=recv[3],
+            dst_ref=recv[3],
+            send_sem=sems.at[0],
+            recv_sem=recv_sem,
+            device_id=z_peers[0][0],
+            device_id_type=MESH,
+        ).wait()
 
     def add(n):
         size = sizes[n + 1]
@@ -468,7 +488,7 @@
         def chunk(i, carry):
             start = i * step
             at = pl.ds(pl.multiple_of(offsets[n + 1] + start, step), step)
-            other = recv[n][pl.ds(pl.multiple_of(start, step), step), :].astype(jnp.float32)
+            other = targets[n][pl.ds(pl.multiple_of(start, step), step), :].astype(jnp.float32)
             part[at, :] = (part[at, :].astype(jnp.float32) + other).astype(part.dtype)
             return carry
 
@@ -481,18 +501,22 @@
         def run():
             copies[n].wait()
             add(n)
-            if n + 1 < len(copies):
+            if n < last:
                 copies[n + 1].start()
-            else:
+            elif z_peers:
                 for copy in spread:
                     copy.start()
+            else:
+                kept.start()
+                back[last].start()
 
         return run
 
     def settle():
-        for copy in spread:
-            copy.wait()
-        others = [recv[3][n].astype(jnp.float32) for n in range(len(spread))]
+        wait_all(sems.at[4])
+        others = [
+            recv[3][pl.ds(n * shard, shard), :].astype(jnp.float32) for n in range(len(spread))
+        ]
         own = part[mine, :].astype(jnp.float32)
         part[mine, :] = ((own + others[0]) + (others[1] + others[2])).astype(part.dtype)
         kept.start()
@@ -501,19 +525,23 @@
 
     def collect():
         kept.wait()
-        for copy in gather:
-            copy.wait()
-        back[-1].start()
+        wait_all(sems.at[9])
+        back[last].start()
 
     def unfold(n):
         def run():
             back[n].wait()
+            if n == last and not z_peers:
+                kept.wait()
             if n > 0:
                 back[n - 1].start()
 
         return run
 
-    return [first] + [fold(n) for n in range(3)] + [settle, collect] + [unfold(n) for n in (2, 1, 0)]
+    steps = [first] + [fold(n) for n in range(last + 1)]
+    if z_peers:
+        steps += [settle, collect]
+    return steps + [unfold(n) for n in range(last, -1, -1)]
 
 
 def small_job(part, total, recv, sems, halves, z_peers):
@@ -527,7 +555,7 @@
                 src_ref=part.at[:, give],
                 dst_ref=recv[n],
                 send_sem=sems.at[0],
-                recv_sem=sems.at[3 + n],
+                recv_sem=sems.at[1 + n],
                 device_id=partner,
                 device_id_type=MESH,
             )
@@ -537,7 +565,7 @@
                 src_ref=total.at[:, keep],
                 dst_ref=total.at[:, keep],
                 send_sem=sems.at[0],
-                recv_sem=sems.at[9 + n],
+                recv_sem=sems.at[6 + n],
                 device_id=partner,
                 device_id_type=MESH,
             )
@@ -549,8 +577,8 @@
         pltpu.make_async_remote_copy(
             src_ref=part.at[:, mine],
             dst_ref=recv[3].at[n],
-            send_sem=sems.at[n],
-            recv_sem=sems.at[6 + n],
+            send_sem=sems.at[0],
+            recv_sem=sems.at[4],
             device_id=peer,
             device_id_type=MESH,
         )
@@ -573,8 +601,14 @@
         return run
 
     def settle():
-        for copy in spread:
-            copy.wait()
+        pltpu.make_async_remote_copy(
+            src_ref=recv[3],
+            dst_ref=recv[3],
+            send_sem=sems.at[0],
+            recv_sem=sems.at[4],
+            device_id=z_peers[0][0],
+            device_id_type=MESH,
+        ).wait()
         total[:, mine] = (part[:, mine] + recv[3][0]) + (recv[3][1] + recv[3][2])
         back[-1].start()
 
@@ -628,7 +662,7 @@
         queries,
         kv,
         attended,
-        stats,
+        log_totals,
         norm1,
         inverse1,
         mid_low,
@@ -637,14 +671,13 @@
         norm2,
         inverse2,
         meta,
-        bias_row,
         bias_col,
         valid,
         ffn_low,
         hidden_low,
         branch_low,
         attended_low,
-        stats_rows,
+        centers,
         dq_t,
         dkv_own,
         dkv_send,
@@ -700,17 +733,24 @@
     def choose(first, second):
         return core * second + (1 - core) * first
 
-    halves = [
-        (peer, core),
-        (
-            (choose(x_next[0], y_next[0]), choose(x_next[1], y_next[1])),
-            choose(x_side, y_side),
-        ),
-        (
-            (choose(y_next[0], x_next[0]), choose(y_next[1], x_next[1])),
-            choose(y_side, x_side),
-        ),
-    ]
+    sides = {
+        "c": (peer, core),
+        "x": (x_next, x_side),
+        "y": (y_next, y_side),
+        "n": (z_peers[0][0], lax.rem(z_side, 2)),
+        "f": (z_peers[1][0], z_side // 2),
+    }
+
+    def both(first, second):
+        if first == second:
+            return sides[first]
+        (one, one_bit), (two, two_bit) = sides[first], sides[second]
+        device = (choose(one[0], two[0]), choose(one[1], two[1]))
+        return device, choose(one_bit, two_bit)
+
+    def path(kind):
+        first, second = PATHS[kind]
+        return [both(*pair) for pair in zip(first, second)]
 
     def partner(k):
         return (t - core + side, block_tables * core + k)
@@ -821,7 +861,6 @@
     meta_copy.wait()
     length = meta[side, pl.ds(slot, 1), :][:, :1]
     train = meta[side, pl.ds(slot + block_tables, 1), :][:, :1]
-    bias_row[...] = jnp.where(lax.broadcasted_iota(jnp.int32, (1, seq), 1) < train, 0.0, MASKED)
     bias_col[...] = jnp.where(lax.broadcasted_iota(jnp.int32, (seq, 1), 0) < train, 0.0, MASKED)
     valid[...] = jnp.where(
         lax.broadcasted_iota(jnp.int32, (rows, 1), 0) + core * rows < length, 1.0, 0.0
@@ -877,29 +916,20 @@
         for h in range(HEADS):
             kv_copy(h).start()
 
-        def attend(step, carry):
-            h = step // tiles
-            at = pl.ds(pl.multiple_of(lax.rem(step, tiles) * TILE, TILE), TILE)
+        def attend(h, carry):
             cols = head_cols(h)
-
-            @pl.when(lax.rem(step, tiles) == 0)
-            def _():
-                kv_copy(h).wait()
-
-            key_rows = kv[layer, h, :, pl.ds(0, head_dim)]
-            value_rows = kv[layer, h, :, pl.ds(head_dim, head_dim)]
-            scores = dot(queries[layer, at, cols], key_rows, NT) + bias_row[...]
-            row_max = jnp.max(scores, axis=-1, keepdims=True)
+            kv_copy(h).wait()
+            scores = dot(kv[layer, h, :, pl.ds(0, head_dim)], queries[layer, :, cols], NT)
+            scores = scores + bias_col[...]
+            row_max = jnp.max(scores, axis=0, keepdims=True)
             exponent = jnp.exp(scores - row_max)
-            total = jnp.sum(exponent, axis=-1, keepdims=True)
-            probs = (exponent * (1.0 / total)).astype(jnp.bfloat16)
-            attended[layer, at, cols] = dot(probs, value_rows).astype(jnp.bfloat16)
-            lane = lax.broadcasted_iota(jnp.int32, (TILE, head_dim), 1)
-            kept = jnp.where(h == 0, jnp.zeros((TILE, head_dim), jnp.float32), stats[layer, at, :])
-            stats[layer, at, :] = jnp.where(lane == h, row_max + jnp.log(total), kept)
+            total = jnp.sum(exponent, axis=0, keepdims=True)
+            mixed = dot(kv[layer, h, :, pl.ds(head_dim, head_dim)], exponent.astype(jnp.bfloat16), TN)
+            attended[layer, :, cols] = jnp.transpose(mixed * (1.0 / total)).astype(jnp.bfloat16)
+            log_totals[layer, pl.ds(h, 1), :] = row_max + jnp.log(total)
             return carry
 
-        lax.fori_loop(0, HEADS * tiles, attend, 0)
+        lax.fori_loop(0, HEADS, attend, 0)
         if layer == 0:
             for load in loads[1:]:
                 load.wait()
@@ -962,7 +992,9 @@
                 jobs[index].pop(0)()
 
     def reduce(part, total, recv):
-        begin(reduce_job(part, total, recv, job_sem.at[len(jobs)], halves, z_peers, z_side))
+        halves = path(KINDS[len(jobs)])
+        peers = z_peers if len(halves) == 3 else []
+        begin(reduce_job(part, total, recv, job_sem.at[len(jobs)], halves, peers, z_side))
 
     def reduce_halves(part, total, recv):
         width = part.shape[1] // HALVES
@@ -971,7 +1003,7 @@
             reduce(
                 part.at[:, cols],
                 total.at[:, cols],
-                [ref.at[:, cols] for ref in recv[:3]] + [recv[3].at[:, :, cols]],
+                [ref.at[:, cols] for ref in recv],
             )
 
     def backward(layer):
@@ -1022,11 +1054,11 @@
             attended_low[at, :] = low
             product = low.astype(jnp.float32) * attended[layer, at, :].astype(jnp.float32)
             lane = lax.broadcasted_iota(jnp.int32, (TILE, head_dim), 1)
-            held = stats[layer, at, :]
+            held = jnp.zeros((TILE, head_dim), jnp.float32)
             for h in range(HEADS):
                 center = jnp.sum(product[:, h * head_dim : (h + 1) * head_dim], axis=-1, keepdims=True)
-                held = jnp.where(lane == HEADS + h, center, held)
-            stats_rows[:, at] = jnp.transpose(held)[: 2 * HEADS, :]
+                held = jnp.where(lane == h, center, held)
+            centers[:, at] = jnp.transpose(held)[:8, :]
 
         each_tile(dense, (tick,) * tiles)
         g_up[layer] = dot(mid_low[layer], hidden_low[...], TN).astype(jnp.bfloat16)
@@ -1046,11 +1078,11 @@
                 query_rows = queries[layer, :, cols]
                 grads = attended_low[:, cols]
                 probs = jnp.exp(
-                    dot(key_rows, query_rows, NT) + bias_col[at, :] - stats_rows[pl.ds(h, 1), :]
+                    dot(key_rows, query_rows, NT) + bias_col[at, :] - log_totals[layer, pl.ds(h, 1), :]
                 )
                 value_part = dot(probs.astype(jnp.bfloat16), grads)
                 probs_grad = dot(kv[layer, h, at, pl.ds(head_dim, head_dim)], grads, NT)
-                scores_low = (probs * (probs_grad - stats_rows[pl.ds(HEADS + h, 1), :])).astype(
+                scores_low = (probs * (probs_grad - centers[pl.ds(h, 1), :])).astype(
                     jnp.bfloat16
                 )
                 key_part = dot(scores_low, query_rows)
@@ -1135,7 +1167,7 @@
                 t_small.at[layer],
                 [ref.at[layer] for ref in recv_small],
                 job_sem.at[len(jobs)],
-                halves,
+                path("A"),
                 z_peers,
             )
         )
@@ -1175,34 +1207,83 @@
     xg_left()
 
 
-def widen_kernel(f_in, f_out, f_up, f_down, f_act, f_xgrad, small, *outs):
-    act, xgrad, in_weight, out_weight, up_weight, down_weight, root_means = outs[:7]
+def widen_kernel(f_in, f_out, f_up, f_down, f_act, f_xgrad, small, *refs):
+    act, xgrad, in_weight, out_weight, up_weight, down_weight, root_means = refs[:7]
+    low = refs[16:22]
+    wide = refs[22:28]
+    read_sem, write_sem = refs[28:]
     groups, width = f_in.shape[1], f_in.shape[3] // 3
-    for group in range(groups):
+    half = f_in.shape[2] // 2
+
+    def table_parts(n, source, target):
+        def convert():
+            for k in range(source.shape[0]):
+                wide[n][:, k, :] = low[n][k].astype(jnp.float32)
+
+        return (source, low[n], convert, wide[n], target)
+
+    def plain_part(n, source, target, layer):
+        def convert():
+            wide[n][layer] = low[n][layer].astype(jnp.float32)
+
+        return (
+            source.at[layer],
+            low[n].at[layer],
+            convert,
+            wide[n].at[layer],
+            target.at[layer],
+        )
+
+    def in_part(layer, start):
+        at = pl.ds(start, half)
+
+        def convert():
+            for group in range(groups):
+                for n in range(3):
+                    wide[2][layer, at, pl.ds((n * groups + group) * width, width)] = low[2][
+                        layer, group, at, pl.ds(n * width, width)
+                    ].astype(jnp.float32)
+
+        return (
+            f_in.at[layer, :, at],
+            low[2].at[layer, :, at],
+            convert,
+            wide[2].at[layer, at],
+            in_weight.at[layer, at],
+        )
+
+    parts = [plain_part(3, f_out, out_weight, layer) for layer in range(LAYERS)]
+    parts += [table_parts(0, f_act, act), table_parts(1, f_xgrad, xgrad)]
+    for layer in range(LAYERS):
+        parts += [plain_part(4, f_up, up_weight, layer), plain_part(5, f_down, down_weight, layer)]
+        parts += [in_part(layer, 0), in_part(layer, half)]
+    reads = [
+        pltpu.make_async_copy(source, target, read_sem.at[n])
+        for n, (source, target, _, _, _) in enumerate(parts)
+    ]
+    writes = [
+        pltpu.make_async_copy(source, target, write_sem.at[n])
+        for n, (_, _, _, source, target) in enumerate(parts)
+    ]
+    for copy in reads:
+        copy.start()
+    for copy, write, part in zip(reads, writes, parts):
+        copy.wait()
+        part[2]()
+        write.start()
+    for ref, row in zip(refs[7:16], (0, 1, 3, 4, 5, 6, 7, 8, 9)):
+        for layer in range(LAYERS):
+            ref[pl.ds(layer, 1), :] = small[layer, pl.ds(row, 1), pl.ds(0, ref.shape[1])]
+    dim = f_act.shape[2]
+    count = small[0, pl.ds(13, 1), pl.ds(0, 1)]
+    for layer in range(LAYERS):
+        sums = jnp.sum(small[layer, pl.ds(8, 8), pl.ds(0, dim)], axis=-1, keepdims=True)
         for n in range(3):
-            in_weight[0, :, pl.ds((n * groups + group) * width, width)] = f_in[
-                0, group, :, pl.ds(n * width, width)
-            ].astype(jnp.float32)
-    out_weight[...] = f_out[...].astype(jnp.float32)
-    up_weight[...] = f_up[...].astype(jnp.float32)
-    down_weight[...] = f_down[...].astype(jnp.float32)
-    for k in range(f_act.shape[0]):
-        act[:, k, :] = f_act[k].astype(jnp.float32)
-        xgrad[:, k, :] = f_xgrad[k].astype(jnp.float32)
-
-    @pl.when(pl.program_id(0) == 0)
-    def _():
-        for ref, row in zip(outs[7:], (0, 1, 3, 4, 5, 6, 7, 8, 9)):
-            for layer in range(LAYERS):
-                ref[pl.ds(layer, 1), :] = small[layer, pl.ds(row, 1), pl.ds(0, ref.shape[1])]
-        dim = f_act.shape[2]
-        count = small[0, pl.ds(13, 1), pl.ds(0, 1)]
-        for layer in range(LAYERS):
-            sums = jnp.sum(small[layer, pl.ds(8, 8), pl.ds(0, dim)], axis=-1, keepdims=True)
-            for n in range(3):
-                root_means[pl.ds(layer, 1), pl.ds(n, 1)] = jnp.sqrt(
-                    sums[2 + n : 3 + n, :] / (count * dim)
-                )
+            root_means[pl.ds(layer, 1), pl.ds(n, 1)] = jnp.sqrt(
+                sums[2 + n : 3 + n, :] / (count * dim)
+            )
+    for write in writes:
+        write.wait()
 
 
 def table_device(tables, row_parts, *operands):
@@ -1244,7 +1325,7 @@
         lead, (height, width) = shape[:-2], shape[-2:]
         return [
             [pltpu.VMEM(lead + (height // n, width), bf16) for n in (2, 4, 8)]
-            + [pltpu.VMEM(lead + (3, height // shards, width), bf16)]
+            + [pltpu.VMEM(lead + (3 * height // shards, width), bf16)]
         ]
 
     act, xgrad, *sums, small = pl.pallas_call(
@@ -1277,7 +1358,7 @@
             pltpu.VMEM((LAYERS, rows, dim), bf16),
             pltpu.VMEM((LAYERS, HEADS, seq, 2 * head_dim), bf16),
             pltpu.VMEM((LAYERS, rows, dim), bf16),
-            pltpu.VMEM((LAYERS, rows, head_dim), f32),
+            pltpu.VMEM((LAYERS, 8, rows), f32),
             pltpu.VMEM((LAYERS, rows, dim), f32),
             pltpu.VMEM((LAYERS, rows, 1), f32),
             pltpu.VMEM((LAYERS, rows, dim), bf16),
@@ -1286,14 +1367,13 @@
             pltpu.VMEM((LAYERS, rows, dim), f32),
             pltpu.VMEM((LAYERS, rows, 1), f32),
             pltpu.VMEM((2, 2 * block_tables, 128), jnp.int32),
-            pltpu.VMEM((1, seq), f32),
             pltpu.VMEM((seq, 1), f32),
             pltpu.VMEM((rows, 1), f32),
             pltpu.VMEM((rows, dim), bf16),
             pltpu.VMEM((rows, hidden), bf16),
             pltpu.VMEM((rows, dim), bf16),
             pltpu.VMEM((rows, dim), bf16),
-            pltpu.VMEM((2 * HEADS, rows), f32),
+            pltpu.VMEM((8, rows), f32),
             pltpu.VMEM((dim, rows), f32),
             pltpu.VMEM((2, rows, 2 * dim // groups), f32),
             pltpu.VMEM((LAYERS, groups, rows, 2 * dim // groups), bf16),
@@ -1315,7 +1395,7 @@
             dma((LAYERS, HEADS, 2)),
             dma((LAYERS, groups, 2)),
             dma((2,)),
-            dma((LAYERS * (2 * HALVES + 2 + groups), 16)),
+            dma((LAYERS * (2 * HALVES + 2 + groups), 12)),
         ],
         compiler_params=pltpu.CompilerParams(
             collective_id=0, has_side_effects=True, vmem_limit_bytes=62 * 1024 * 1024
@@ -1339,23 +1419,6 @@
         ffn_gain,
         ffn_shift,
     )
-    steps = 4
-
-    def whole(shape):
-        return pl.BlockSpec(shape, lambda l, i: (0,) * len(shape))
-
-    def sliced(height, width):
-        return pl.BlockSpec((1, height // steps, width), lambda l, i: (l, i, 0))
-
-    weights = [
-        sliced(dim, 3 * dim),
-        sliced(dim, dim),
-        sliced(dim, hidden),
-        sliced(hidden, dim),
-    ]
-    cut = local // (LAYERS * steps)
-    table_rows = pl.BlockSpec((block_tables, cut, dim), lambda l, i: (0, l * steps + i, 0))
-    row_tables = pl.BlockSpec((cut, block_tables, dim), lambda l, i: (l * steps + i, 0, 0))
     vector = jax.ShapeDtypeStruct((LAYERS, dim), f32)
     wide_vector = jax.ShapeDtypeStruct((LAYERS, hidden), f32)
     shapes = [
@@ -1369,16 +1432,25 @@
     ] + [vector] * 5 + [wide_vector] + [vector] * 3
     outs = pl.pallas_call(
         widen_kernel,
-        grid=(LAYERS, steps),
         out_shape=shapes,
-        in_specs=[
-            pl.BlockSpec((1, groups, dim // steps, 3 * dim // groups), lambda l, i: (l, 0, i, 0)),
-            *weights[1:],
-            table_rows,
-            table_rows,
-            whole((LAYERS, 16, hidden)),
-        ],
-        out_specs=[row_tables, row_tables, *weights] + [whole(s.shape) for s in shapes[6:]],
+        in_specs=[hbm] * 6 + [vmem],
+        out_specs=[hbm] * 6 + [vmem] * 10,
+        scratch_shapes=[
+            pltpu.VMEM(shape, dtype)
+            for dtype, in_shape, rows_shape in (
+                (bf16, in_part, block),
+                (f32, in_weight.shape, tables_in.shape),
+            )
+            for shape in (
+                rows_shape,
+                rows_shape,
+                in_shape,
+                out_weight.shape,
+                up_weight.shape,
+                down_weight.shape,
+            )
+        ]
+        + [dma((5 * LAYERS + 2,))] * 2,
         compiler_params=pltpu.CompilerParams(vmem_limit_bytes=62 * 1024 * 1024),
     )(*sums, act, xgrad, small)
     act, xgrad, g_in, g_out, g_up, g_down, root_means = outs[:7]

time: 167 us -> 161 us (0.964)
  Pallas kernels: 163 us -> 157 us
    pallas_call x1, Pallas kernels: 152 us -> 147 us  [table_device(): pl.pallas_call(functools.partial(table_kernel, local, block_tables, seq),...]
where the time goes in v4:
time: 161 us
  Pallas kernels  157 us (98%)
  local copies, waits for them, and re-layouts  2.37 us (1%)
    pallas_call x1, Pallas kernels, table_device(): pl.pallas_call(functools.partial(table_kernel, local, block_tables, seq),...  147 us
    pallas_call x1, Pallas kernels, table_device(): pl.pallas_call(widen_kernel, out_shape=shapes, in_specs=[hbm] * 6 + [vmem...  10.8 us

profile of v4, /device:TPU:0, one launch (start us, length us, event | category | flops | bytes accessed | tf_op | source)
XLA Modules:
  0.0 160.7 jit_solution(8599388346393788087)
XLA Ops:
  0.6 2.4 %copy_bitcast_fusion = (bf16[4,128,512]{2,1,0:T(8,128)(2,1)}, bf16[4,128,512]{2,1,0:T(8,128)(2,1)}) fusion(bf16[128,4,512]{2,1,0:T(4,128)(2,1)} %param.31, bf16[128,4,512]{2,1,0:T(4,128)(2,1)} %param.17), kind=kLoop, calls=%fused_computation | loop fusion | bytes 2097152 | tf_op jit(solution)/shard_map/transpose | solution.py:1405
  3.0 146.7 %shard_map.288 = (bf16[4,128,512]{2,1,0:T(8,128)(2,1)}, bf16[4,128,512]{2,1,0:T(8,128)(2,1)}, bf16[2,4,512,384]{3,2,1,0:T(8,128)(2,1)}, bf16[2,512,512]{2,1,0:T(...) custom-call(bf16[4,128,512]{2,1,0:T(8,128)(2,1)} %get-tuple-element.63.x_hbm, ...), custom_call_target="tpu_custom_call" | custom-call | tf_op jit(solution)/shard_map/pallas_call | solution.py:1331
  149.7 10.8 %shard_map.289 = (f32[128,4,512]{2,1,0:T(4,128)}, f32[128,4,512]{2,1,0:T(4,128)}, f32[2,512,1536]{2,1,0:T(8,128)}, f32[2,512,512]{2,1,0:T(8,128)}, f32[2,512,102...) custom-call(bf16[2,4,512,384]{3,2,1,0:T(8,128)(2,1)} %get-tuple-elem, ...), custom_call_target="tpu_custom_call" | custom-call | tf_op jit(solution)/shard_map/pallas_call | solution.py:1433

commit v5 on v4

--- a/solution.py
+++ b/solution.py
@@ -1,4 +1,5 @@
 import functools
+import math
 
 import jax
 import jax.numpy as jnp
@@ -339,59 +340,49 @@
 NT = (((1,), (1,)), ((), ()))
 NN = (((1,), (0,)), ((), ()))
 TN = (((0,), (0,)), ((), ()))
-TILE = 256
+TILE = 512
 VECTORS = 9
-GROUPS = 4
+GROUPS = (4, 2)
 HALVES = 2
 PATHS = {
-    "A": ("cxy", "cyx"),
+    "A": ("cxyz", "cyxz"),
+    "B": ("cxynf", "cyxnf"),
     "N": ("cnyxf", "cnyxf"),
-    "P": ("cxynf", "cxynf"),
-    "Q": ("cyxnf", "cyxnf"),
+    "D": ("cdz", "cdz"),
 }
-KINDS = "NAAAQNAANAQPANANAAAA"
+KINDS = "ABNANBBAANDAD"
 SCHEDULE = (
     (),
     (),
-    (0, 1),
+    (0,),
+    (),
+    (),
+    (),
+    (1, 2),
+    (0,),
+    (3,),
+    (),
+    (1,),
+    (0, 2, 3, 4, 5, 1),
     (),
     (),
     (),
     (),
     (),
-    (2, 1, 3, 4),
     (),
-    (0, 5),
+    (2, 3, 0, 1, 6, 7, 8),
+    (5,),
     (),
+    (2,),
+    (4, 9),
     (),
+    (1,),
     (),
-    (1, 6),
-    (),
-    (5, 7),
-    (0, 1, 2, 3, 4, 8, 9),
-    (5, 6),
-    (0, 1, 7),
-    (8, 9, 10, 11, 2, 5, 3, 4),
-    (0, 6),
-    (1, 7),
-    (9,),
-    (),
-    (8, 5, 12, 13, 14),
-    (11, 4, 10),
-    (1,),
-    (0, 8, 9, 15, 2),
-    (1, 3, 5, 6, 7, 4),
-    (12, 11, 13),
-    (0, 8, 9, 10, 14, 5, 16),
-    (),
-    (),
-    (12, 17),
-    (2, 4, 6, 7, 8, 9, 11, 3, 13, 10, 18, 19),
     (
-        5, 15, 0, 14, 12, 16, 4, 11, 10, 8, 17, 9, 13, 2, 6, 19, 7, 9, 15, 3, 11, 16, 10, 14, 8, 12,
-        13, 4, 19, 5, 17, 18, 15, 5, 11, 13, 19, 6, 12, 7, 0, 10, 15, 18, 16, 2, 4, 3, 14, 17, 6,
-        19, 7, 13, 11, 8, 0, 15, 2, 4, 3, 8, 10, 19, 18, 16, 13, 17, 14, 15, 12, 19, 18, 12, 19, 16,
-        17, 11, 15, 13, 10, 18, 11, 14, 13, 10, 16, 17, 14, 15, 18, 16, 17, 15, 18,
+        10, 12, 3, 8, 11, 1, 6, 9, 0, 2, 5, 4, 12, 2, 8, 7, 5, 9, 12, 11, 1, 10, 8, 3, 6, 4, 2, 9,
+        0, 5, 12, 10, 8, 11, 1, 7, 9, 4, 6, 5, 10, 2, 3, 9, 11, 4, 6, 7, 5, 9, 12, 13, 8, 11, 6, 3,
+        4, 9, 5, 2, 7, 10, 1, 12, 11, 0, 6, 8, 4, 9, 7, 3, 2, 11, 10, 6, 5, 4, 11, 8, 7, 0, 1, 5, 6,
+        7, 9, 4, 6,
     ),
 )
 
@@ -408,219 +399,154 @@
     return jnp.mean(values, axis=-1, keepdims=True)
 
 
-def reduce_job(part, total, recv, sems, halves, z_peers, quarter):
-    rows = part.shape[0]
-    shard = recv[3].shape[0] // 3
-    offsets, sizes, copies, back = [0], [rows], [], []
-    targets = recv[:3] + [recv[3].at[pl.ds(0, 2 * shard)], recv[3].at[pl.ds(2 * shard, shard)]]
-    for n, (partner, bit) in enumerate(halves):
-        size = sizes[-1] // 2
-        keep = pl.multiple_of(offsets[-1] + bit * size, size)
-        give = pl.multiple_of(offsets[-1] + (1 - bit) * size, size)
-        copies.append(
-            pltpu.make_async_remote_copy(
-                src_ref=part.at[pl.ds(give, size)],
-                dst_ref=targets[n],
-                send_sem=sems.at[0],
-                recv_sem=sems.at[1 + n],
-                device_id=partner,
-                device_id_type=MESH,
-            )
-        )
-        offsets.append(keep)
-        sizes.append(size)
-        held = part if size == shard else total
-        back.append(
-            pltpu.make_async_remote_copy(
-                src_ref=held.at[pl.ds(keep, size)],
-                dst_ref=total.at[pl.ds(keep, size)],
-                send_sem=sems.at[0],
-                recv_sem=sems.at[6 + n],
-                device_id=partner,
-                device_id_type=MESH,
-            )
-        )
-    last = len(halves) - 1
-    base = offsets[-1]
-
-    def piece(index):
-        return pl.ds(pl.multiple_of(base + index * shard, shard), shard)
-
-    mine = piece(quarter if z_peers else 0)
-    spread, gather = [], []
-    for n, (peer, index) in enumerate(z_peers):
+def send(source, target, sems, stage, device):
+    return pltpu.make_async_remote_copy(
+        src_ref=source,
+        dst_ref=target,
+        send_sem=sems.at[0],
+        recv_sem=sems.at[1 + stage],
+        device_id=device,
+        device_id_type=MESH,
+    )
+
+
+def reduce_job(part, total, recv, sems, stages):
+    rows, used = part.shape[0], 0
+    base, height = 0, rows
+    spread, gather, inbox, held = [], [], [], []
+    last = len(stages) - 1
+    for n, (own, peers) in enumerate(stages):
+        height = height // (len(peers) + 1)
+
+        def piece(index):
+            return pl.ds(pl.multiple_of(base + index * height, height), height)
+
+        mine = piece(own)
+        inbox.append(recv.at[pl.ds(used, len(peers) * height)])
         spread.append(
-            pltpu.make_async_remote_copy(
-                src_ref=part.at[piece(index)],
-                dst_ref=recv[3].at[pl.ds(n * shard, shard)],
-                send_sem=sems.at[0],
-                recv_sem=sems.at[4],
-                device_id=peer,
-                device_id_type=MESH,
-            )
-        )
+            [
+                send(part.at[piece(index)], recv.at[pl.ds(used + m * height, height)], sems, n, device)
+                for m, (device, index) in enumerate(peers)
+            ]
+        )
+        source = part if n == last else total
         gather.append(
-            pltpu.make_async_remote_copy(
-                src_ref=part.at[mine],
-                dst_ref=total.at[mine],
-                send_sem=sems.at[0],
-                recv_sem=sems.at[9],
-                device_id=peer,
-                device_id_type=MESH,
-            )
-        )
+            [send(source.at[mine], total.at[mine], sems, 5 + n, device) for device, _ in peers]
+        )
+        held.append((base + own * height, height, used, len(peers)))
+        used += len(peers) * height
+        base = base + own * height
     kept = pltpu.make_async_copy(part.at[mine], total.at[mine], sems.at[11])
 
-    def wait_all(recv_sem):
-        pltpu.make_async_remote_copy(
-            src_ref=recv[3],
-            dst_ref=recv[3],
-            send_sem=sems.at[0],
-            recv_sem=recv_sem,
-            device_id=z_peers[0][0],
-            device_id_type=MESH,
-        ).wait()
+    def wait_all(stage, n):
+        send(inbox[n], inbox[n], sems, stage, stages[n][1][0][0]).wait()
+
+    def start_all(copies):
+        for copy in copies:
+            copy.start()
 
     def add(n):
-        size = sizes[n + 1]
-        step = min(size, 128)
+        start, size, offset, count = held[n]
+        step = 128 if size % 128 == 0 else size
 
         def chunk(i, carry):
-            start = i * step
-            at = pl.ds(pl.multiple_of(offsets[n + 1] + start, step), step)
-            other = targets[n][pl.ds(pl.multiple_of(start, step), step), :].astype(jnp.float32)
-            part[at, :] = (part[at, :].astype(jnp.float32) + other).astype(part.dtype)
+            at = pl.ds(pl.multiple_of(start + i * step, step), step)
+            sums = part[at, :].astype(jnp.float32)
+            for m in range(count):
+                other = pl.ds(pl.multiple_of(offset + m * size + i * step, 16), step)
+                sums = sums + recv[other, :].astype(jnp.float32)
+            part[at, :] = sums.astype(part.dtype)
             return carry
 
         lax.fori_loop(0, size // step, chunk, 0)
 
     def first():
-        copies[0].start()
+        start_all(spread[0])
 
     def fold(n):
         def run():
-            copies[n].wait()
+            wait_all(n, n)
             add(n)
             if n < last:
-                copies[n + 1].start()
-            elif z_peers:
-                for copy in spread:
-                    copy.start()
+                start_all(spread[n + 1])
             else:
                 kept.start()
-                back[last].start()
+                start_all(gather[n])
 
         return run
-
-    def settle():
-        wait_all(sems.at[4])
-        others = [
-            recv[3][pl.ds(n * shard, shard), :].astype(jnp.float32) for n in range(len(spread))
-        ]
-        own = part[mine, :].astype(jnp.float32)
-        part[mine, :] = ((own + others[0]) + (others[1] + others[2])).astype(part.dtype)
-        kept.start()
-        for copy in gather:
-            copy.start()
-
-    def collect():
-        kept.wait()
-        wait_all(sems.at[9])
-        back[last].start()
 
     def unfold(n):
         def run():
-            back[n].wait()
-            if n == last and not z_peers:
+            wait_all(5 + n, n)
+            if n == last:
                 kept.wait()
             if n > 0:
-                back[n - 1].start()
+                start_all(gather[n - 1])
 
         return run
 
-    steps = [first] + [fold(n) for n in range(last + 1)]
-    if z_peers:
-        steps += [settle, collect]
-    return steps + [unfold(n) for n in range(last, -1, -1)]
-
-
-def small_job(part, total, recv, sems, halves, z_peers):
-    offset, size, copies, back, kept_cols = 0, part.shape[1], [], [], []
-    for n, (partner, bit) in enumerate(halves):
-        size = size // 2
-        keep = pl.ds(pl.multiple_of(offset + bit * size, size), size)
-        give = pl.ds(pl.multiple_of(offset + (1 - bit) * size, size), size)
-        copies.append(
-            pltpu.make_async_remote_copy(
-                src_ref=part.at[:, give],
-                dst_ref=recv[n],
-                send_sem=sems.at[0],
-                recv_sem=sems.at[1 + n],
-                device_id=partner,
-                device_id_type=MESH,
-            )
-        )
-        back.append(
-            pltpu.make_async_remote_copy(
-                src_ref=total.at[:, keep],
-                dst_ref=total.at[:, keep],
-                send_sem=sems.at[0],
-                recv_sem=sems.at[6 + n],
-                device_id=partner,
-                device_id_type=MESH,
-            )
-        )
-        kept_cols.append(keep)
-        offset = offset + bit * size
-    mine = kept_cols[-1]
-    spread = [
-        pltpu.make_async_remote_copy(
-            src_ref=part.at[:, mine],
-            dst_ref=recv[3].at[n],
-            send_sem=sems.at[0],
-            recv_sem=sems.at[4],
-            device_id=peer,
-            device_id_type=MESH,
-        )
-        for n, (peer, _) in enumerate(z_peers)
-    ]
+    return [first] + [fold(n) for n in range(last + 1)] + [unfold(n) for n in range(last, -1, -1)]
+
+
+def small_job(part, total, recv, sems, stages):
+    base, width = 0, part.shape[1]
+    spread, gather, held = [], [], []
+    last = len(stages) - 1
+    for n, (own, peers) in enumerate(stages):
+        if n < last:
+            width = width // (len(peers) + 1)
+
+        def piece(index):
+            return pl.ds(pl.multiple_of(base + index * width, width), width)
+
+        mine = piece(own) if n < last else piece(0)
+        spread.append(
+            [
+                send(part.at[:, piece(index) if n < last else mine], recv[n].at[m], sems, n, device)
+                for m, (device, index) in enumerate(peers)
+            ]
+        )
+        gather.append(
+            [send(total.at[:, mine], total.at[:, mine], sems, 5 + n, device) for device, _ in peers]
+        )
+        held.append(mine)
+        if n < last:
+            base = base + own * width
+
+    def wait_all(stage, n):
+        send(recv[n], recv[n], sems, stage, stages[n][1][0][0]).wait()
+
+    def start_all(copies):
+        for copy in copies:
+            copy.start()
 
     def first():
-        copies[0].start()
+        start_all(spread[0])
 
     def fold(n):
         def run():
-            copies[n].wait()
-            part[:, kept_cols[n]] = part[:, kept_cols[n]] + recv[n][...]
-            if n + 1 < len(copies):
-                copies[n + 1].start()
+            wait_all(n, n)
+            own = part[:, held[n]]
+            if n < last:
+                for m in range(len(stages[n][1])):
+                    own = own + recv[n][m]
+                part[:, held[n]] = own
+                start_all(spread[n + 1])
             else:
-                for copy in spread:
-                    copy.start()
+                total[:, held[n]] = (own + recv[n][0]) + (recv[n][1] + recv[n][2])
+                start_all(gather[n - 1])
 
         return run
-
-    def settle():
-        pltpu.make_async_remote_copy(
-            src_ref=recv[3],
-            dst_ref=recv[3],
-            send_sem=sems.at[0],
-            recv_sem=sems.at[4],
-            device_id=z_peers[0][0],
-            device_id_type=MESH,
-        ).wait()
-        total[:, mine] = (part[:, mine] + recv[3][0]) + (recv[3][1] + recv[3][2])
-        back[-1].start()
 
     def unfold(n):
         def run():
-            back[n].wait()
+            wait_all(5 + n, n)
             if n > 0:
-                back[n - 1].start()
+                start_all(gather[n - 1])
 
         return run
 
-    return [first] + [fold(n) for n in range(3)] + [settle] + [unfold(n) for n in (2, 1, 0)]
+    return [first] + [fold(n) for n in range(last + 1)] + [unfold(n) for n in range(last - 1, -1, -1)]
 
 
 def table_kernel(
@@ -641,9 +567,9 @@
     (
         act_hbm,
         xgrad_hbm,
-        t_in,
-        t_out,
-        t_up,
+        t_in_first,
+        t_in_last,
+        t_mid,
         t_down,
         t_small,
         w_in,
@@ -651,9 +577,9 @@
         w_up,
         w_down,
         vectors,
-        g_in,
-        g_out,
-        g_up,
+        g_in_first,
+        g_in_last,
+        g_mid,
         g_down,
         small,
         in_low,
@@ -674,19 +600,16 @@
         bias_col,
         valid,
         ffn_low,
-        hidden_low,
-        branch_low,
         attended_low,
         centers,
-        dq_t,
-        dkv_own,
         dkv_send,
-        dkv_recv,
+        dkv_recv_first,
+        dkv_recv_last,
         proj_low,
         staged,
-        recv_in,
-        recv_out,
-        recv_up,
+        recv_in_first,
+        recv_in_last,
+        recv_mid,
         recv_down,
         recv_small,
         x_send,
@@ -704,13 +627,14 @@
         job_sem,
     ) = refs
     upstream = stream
+    t_in, g_in, recv_in = (t_in_first, t_in_last), (g_in_first, g_in_last), (recv_in_first, recv_in_last)
+    branch_low = ffn_low
+    dkv_recvs = (dkv_recv_first, dkv_recv_last)
     rows = block_tables * local
     dim = in_low.shape[-1]
     head_dim = dim // HEADS
     scale = head_dim**-0.5
     tiles = rows // TILE
-    group_heads = HEADS // GROUPS
-    group_width = group_heads * head_dim
     t = lax.axis_index("tables")
     r = lax.axis_index("rows")
     core = lax.rem(t, 2)
@@ -733,20 +657,29 @@
     def choose(first, second):
         return core * second + (1 - core) * first
 
+    y_index = t + 2 - 4 * y_side
+    corner = x_side + 2 * y_side
+    corners = [
+        (x_next, 1 - x_side + 2 * y_side),
+        (y_next, x_side + 2 - 2 * y_side),
+        ((y_index, x_next[1]), 3 - corner),
+    ]
     sides = {
-        "c": (peer, core),
-        "x": (x_next, x_side),
-        "y": (y_next, y_side),
-        "n": (z_peers[0][0], lax.rem(z_side, 2)),
-        "f": (z_peers[1][0], z_side // 2),
+        "c": (core, [(peer, 1 - core)]),
+        "x": (x_side, [(x_next, 1 - x_side)]),
+        "y": (y_side, [(y_next, 1 - y_side)]),
+        "n": (lax.rem(z_side, 2), [(z_peers[0][0], 1 - lax.rem(z_side, 2))]),
+        "f": (z_side // 2, [(z_peers[1][0], 1 - z_side // 2)]),
+        "d": (corner, corners),
+        "z": (z_side, z_peers),
     }
 
     def both(first, second):
         if first == second:
             return sides[first]
-        (one, one_bit), (two, two_bit) = sides[first], sides[second]
+        (one_own, [(one, one_index)]), (two_own, [(two, two_index)]) = sides[first], sides[second]
         device = (choose(one[0], two[0]), choose(one[1], two[1]))
-        return device, choose(one_bit, two_bit)
+        return choose(one_own, two_own), [(device, choose(one_index, two_index))]
 
     def path(kind):
         first, second = PATHS[kind]
@@ -786,8 +719,8 @@
         def kept(k):
             return pltpu.make_async_copy(source(k), target(k), own_sem)
 
-        def start():
-            for k in range(block_tables):
+        def start(blocks=range(block_tables)):
+            for k in blocks:
 
                 @pl.when(is_self(k))
                 def _():
@@ -865,7 +798,7 @@
     valid[...] = jnp.where(
         lax.broadcasted_iota(jnp.int32, (rows, 1), 0) + core * rows < length, 1.0, 0.0
     )
-    small[0, pl.ds(13, 1), pl.ds(0, 128)] = jnp.broadcast_to(column_sum(valid[...]), (1, 128))
+    small[pl.ds(13, 1), pl.ds(0, 128)] = jnp.broadcast_to(column_sum(valid[...]), (1, 128))
     x_arrive()
     cot_start()
     loads[0].wait()
@@ -874,7 +807,7 @@
         return vectors[pl.ds(layer * VECTORS + index, 1), pl.ds(0, width)]
 
     def add_small(layer, index, values):
-        at = (layer, pl.ds(index, 1), pl.ds(0, values.shape[-1]))
+        at = (pl.ds(layer * 16 + index, 1), pl.ds(0, values.shape[-1]))
         small[at] = small[at] + values
 
     def each_tile(body, after=()):
@@ -992,9 +925,7 @@
                 jobs[index].pop(0)()
 
     def reduce(part, total, recv):
-        halves = path(KINDS[len(jobs)])
-        peers = z_peers if len(halves) == 3 else []
-        begin(reduce_job(part, total, recv, job_sem.at[len(jobs)], halves, peers, z_side))
+        begin(reduce_job(part, total, recv, job_sem.at[len(jobs)], path(KINDS[len(jobs)])))
 
     def reduce_halves(part, total, recv):
         width = part.shape[1] // HALVES
@@ -1003,12 +934,19 @@
             reduce(
                 part.at[:, cols],
                 total.at[:, cols],
-                [ref.at[:, cols] for ref in recv],
+                recv.at[:, cols],
             )
 
     def backward(layer):
-        def recv_of(refs):
-            return [ref.at[layer] for ref in refs]
+        groups = GROUPS[layer]
+        group_heads = HEADS // groups
+        group_width = group_heads * head_dim
+        dkv_recv = dkv_recvs[layer]
+        dq_t = slope.at[layer, :, pl.ds(0, dim)]
+
+        def send_cols(group):
+            return pl.ds(group * 2 * group_width, 2 * group_width)
+
 
         def enter(at):
             if layer == LAYERS - 1:
@@ -1030,13 +968,13 @@
         each_tile(enter)
         g_down[layer] = dot(act_low[layer], ffn_low[...], TN).astype(jnp.bfloat16)
         tick()
-        reduce_halves(g_down.at[layer], t_down.at[layer], recv_of(recv_down))
+        reduce(g_down.at[layer], t_down.at[layer], recv_down.at[layer])
 
         def dense(at):
             hidden = (dot(ffn_low[at, :], w_down[layer], NT) * slope[layer, at, :]).astype(
                 jnp.bfloat16
             )
-            hidden_low[at, :] = hidden
+            proj_low[at, pl.ds(0, hidden.shape[1])] = hidden
             add_small(layer, 6, column_sum(hidden.astype(jnp.float32)))
             first = upstream[at, :] + dot(hidden, w_up[layer], NT)
             normed = norm1[layer, at, :]
@@ -1061,12 +999,14 @@
             centers[:, at] = jnp.transpose(held)[:8, :]
 
         each_tile(dense, (tick,) * tiles)
-        g_up[layer] = dot(mid_low[layer], hidden_low[...], TN).astype(jnp.bfloat16)
+        up_grad = dot(mid_low[layer], proj_low[:, pl.ds(0, 2 * dim)], TN).astype(jnp.bfloat16)
+        g_mid[layer, pl.ds(0, dim), :] = up_grad[:, :dim]
+        g_mid[layer, pl.ds(dim, dim), :] = up_grad[:, dim:]
+        g_mid[layer, pl.ds(2 * dim, dim), :] = dot(attended[layer], branch_low[...], TN).astype(
+            jnp.bfloat16
+        )
         tick()
-        reduce_halves(g_up.at[layer], t_up.at[layer], recv_of(recv_up))
-        g_out[layer] = dot(attended[layer], branch_low[...], TN).astype(jnp.bfloat16)
-        tick()
-        reduce(g_out.at[layer], t_out.at[layer], recv_of(recv_out))
+        reduce_halves(g_mid.at[layer], t_mid.at[layer], recv_mid.at[layer])
 
         def attend(group, base, first, keep):
             def step(i, carry):
@@ -1105,12 +1045,15 @@
 
         def dkv_copy(group):
             return swap(
-                dkv_send.at[layer, group], dkv_recv.at[layer, group], dkv_sem.at[layer, group]
+                dkv_send.at[:, send_cols(group)], dkv_recv.at[group], dkv_sem.at[layer, group]
             )
 
         def attend_peer(group):
             def keep(at, cols, part):
-                dkv_send[layer, group, at, cols] = part.astype(jnp.bfloat16)
+                start = group * 2 * group_width + cols.start
+                dkv_send[at, pl.ds(pl.multiple_of(start, head_dim), cols.size)] = part.astype(
+                    jnp.bfloat16
+                )
 
             attend(group, peer_rows, True, keep)
             dkv_copy(group).start()
@@ -1118,7 +1061,8 @@
 
         def attend_own(group):
             def keep(at, cols, part):
-                dkv_own[group % 2, at, cols] = part
+                start = pl.multiple_of(dim + cols.start, head_dim)
+                slope[layer, at, pl.ds(start, cols.size)] = part
 
             attend(group, own_rows, False, keep)
             tick()
@@ -1130,67 +1074,59 @@
                 group_rows = pl.ds(group * group_width, group_width)
                 query = jnp.transpose(dq_t[group_rows, at]).astype(jnp.bfloat16)
                 pair = (
-                    dkv_own[group % 2, at, :] + dkv_recv[layer, group, at, :].astype(jnp.float32)
+                    slope[layer, at, pl.ds(dim, 2 * group_width)] + dkv_recv[group, at, :].astype(jnp.float32)
                 ).astype(jnp.bfloat16)
-                proj_low[group, at, pl.ds(0, group_width)] = query
-                proj_low[group, at, pl.ds(group_width, 2 * group_width)] = pair
+                for n, part in enumerate((query, pair[:, :group_width], pair[:, group_width:])):
+                    proj_low[at, pl.ds(n * dim + group * group_width, group_width)] = part
                 cols = pl.ds(group * group_width, group_width)
-                small[layer, pl.ds(0, 1), cols] += column_sum(query.astype(jnp.float32)) * scale
-                small[layer, pl.ds(1, 1), cols] += column_sum(
+                small[pl.ds(layer * 16, 1), cols] += column_sum(query.astype(jnp.float32)) * scale
+                small[pl.ds(layer * 16 + 1, 1), cols] += column_sum(
                     pair[:, group_width:].astype(jnp.float32)
                 )
 
             each_tile(finish)
-            grad = dot(in_low[layer], proj_low[group], TN)
-            g_in[layer, group, :, pl.ds(0, group_width)] = (grad[:, :group_width] * scale).astype(
+            parts = [
+                proj_low[:, pl.ds(n * dim + group * group_width, group_width)] for n in range(3)
+            ]
+            grad = dot(in_low[layer], jnp.concatenate(parts, axis=1), TN)
+            g_in[layer][group, :, pl.ds(0, group_width)] = (grad[:, :group_width] * scale).astype(
                 jnp.bfloat16
             )
-            g_in[layer, group, :, pl.ds(group_width, 2 * group_width)] = grad[
+            g_in[layer][group, :, pl.ds(group_width, 2 * group_width)] = grad[
                 :, group_width:
             ].astype(jnp.bfloat16)
             tick()
             reduce(
-                g_in.at[layer, group],
-                t_in.at[layer, group],
-                [ref.at[layer, group] for ref in recv_in],
-            )
-
-        for group in range(GROUPS):
+                g_in[layer].at[group],
+                t_in[layer].at[group],
+                recv_in[layer].at[group],
+            )
+
+        for group in range(groups):
             attend_peer(group)
             if group > 0:
                 finish_group(group - 1)
             attend_own(group)
-        finish_group(GROUPS - 1)
-        begin(
-            small_job(
-                small.at[layer],
-                t_small.at[layer],
-                [ref.at[layer] for ref in recv_small],
-                job_sem.at[len(jobs)],
-                path("A"),
-                z_peers,
-            )
-        )
+        finish_group(groups - 1)
+        if layer == 0:
+            begin(small_job(small, t_small, recv_small, job_sem.at[len(jobs)], path("D")))
 
         def pass_down(at):
-            grad = upstream[at, :]
-            for group in range(GROUPS):
-                for n in range(3):
-                    part = dot(
-                        proj_low[group, at, pl.ds(n * group_width, group_width)],
-                        w_in[layer, :, pl.ds(n * dim + group * group_width, group_width)],
-                        NT,
-                    )
-                    grad = grad + (part * scale if n == 0 else part)
+            grad = (
+                upstream[at, :]
+                + dot(proj_low[at, pl.ds(0, dim)], w_in[layer, :, pl.ds(0, dim)], NT) * scale
+                + dot(proj_low[at, pl.ds(dim, 2 * dim)], w_in[layer, :, pl.ds(dim, 2 * dim)], NT)
+            )
             if layer > 0:
                 upstream[at, :] = grad
             else:
                 staged[1, at, :] = grad.astype(jnp.bfloat16)
 
         each_tile(pass_down)
+        if layer == 0:
+            xg_start(range(block_tables // 2))
+            jobs.append([lambda: xg_start(range(block_tables // 2, block_tables))])
         tick()
-        if layer == 0:
-            xg_start()
 
     for layer in reversed(range(LAYERS)):
         backward(layer)
@@ -1207,77 +1143,91 @@
     xg_left()
 
 
-def widen_kernel(f_in, f_out, f_up, f_down, f_act, f_xgrad, small, *refs):
+def widen_kernel(f_first, f_last, f_mid, f_down, f_act, f_xgrad, small, *refs):
     act, xgrad, in_weight, out_weight, up_weight, down_weight, root_means = refs[:7]
-    low = refs[16:22]
-    wide = refs[22:28]
+    low_act, low_xgrad, low_first, low_last, low_mid, low_down = refs[16:22]
+    wide_act, wide_xgrad, wide_in, wide_out, wide_up, wide_down = refs[22:28]
     read_sem, write_sem = refs[28:]
-    groups, width = f_in.shape[1], f_in.shape[3] // 3
-    half = f_in.shape[2] // 2
-
-    def table_parts(n, source, target):
+    dim = f_act.shape[2]
+    half = dim // 2
+
+    def widened(values):
+        return values.astype(jnp.float32)
+
+    def table_part(source, low, wide, target):
         def convert():
             for k in range(source.shape[0]):
-                wide[n][:, k, :] = low[n][k].astype(jnp.float32)
-
-        return (source, low[n], convert, wide[n], target)
-
-    def plain_part(n, source, target, layer):
+                wide[:, k, :] = widened(low[k])
+
+        return (source, low), convert, [(wide, target)]
+
+    def down_part(layer):
         def convert():
-            wide[n][layer] = low[n][layer].astype(jnp.float32)
+            wide_down[layer] = widened(low_down[layer])
 
         return (
-            source.at[layer],
-            low[n].at[layer],
+            (f_down.at[layer], low_down.at[layer]),
             convert,
-            wide[n].at[layer],
-            target.at[layer],
-        )
-
-    def in_part(layer, start):
+            [(wide_down.at[layer], down_weight.at[layer])],
+        )
+
+    def mid_part(layer):
+        def convert():
+            for n in range(2):
+                wide_up[layer, :, pl.ds(n * dim, dim)] = widened(low_mid[layer, pl.ds(n * dim, dim), :])
+            wide_out[layer] = widened(low_mid[layer, pl.ds(2 * dim, dim), :])
+
+        return (
+            (f_mid.at[layer], low_mid.at[layer]),
+            convert,
+            [
+                (wide_up.at[layer], up_weight.at[layer]),
+                (wide_out.at[layer], out_weight.at[layer]),
+            ],
+        )
+
+    def in_part(layer, source, low, start):
         at = pl.ds(start, half)
+        groups, width = source.shape[0], source.shape[2] // 3
 
         def convert():
             for group in range(groups):
                 for n in range(3):
-                    wide[2][layer, at, pl.ds((n * groups + group) * width, width)] = low[2][
-                        layer, group, at, pl.ds(n * width, width)
-                    ].astype(jnp.float32)
+                    wide_in[layer, at, pl.ds((n * groups + group) * width, width)] = widened(
+                        low[group, at, pl.ds(n * width, width)]
+                    )
 
         return (
-            f_in.at[layer, :, at],
-            low[2].at[layer, :, at],
+            (source.at[:, at], low.at[:, at]),
             convert,
-            wide[2].at[layer, at],
-            in_weight.at[layer, at],
-        )
-
-    parts = [plain_part(3, f_out, out_weight, layer) for layer in range(LAYERS)]
-    parts += [table_parts(0, f_act, act), table_parts(1, f_xgrad, xgrad)]
-    for layer in range(LAYERS):
-        parts += [plain_part(4, f_up, up_weight, layer), plain_part(5, f_down, down_weight, layer)]
-        parts += [in_part(layer, 0), in_part(layer, half)]
+            [(wide_in.at[layer, at], in_weight.at[layer, at])],
+        )
+
+    parts = [
+        table_part(f_act, low_act, wide_act, act),
+        table_part(f_xgrad, low_xgrad, wide_xgrad, xgrad),
+    ]
+    for layer, (source, low) in enumerate(((f_first, low_first), (f_last, low_last))):
+        parts += [in_part(layer, source, low, 0), in_part(layer, source, low, half)]
+        parts += [mid_part(layer), down_part(layer)]
     reads = [
-        pltpu.make_async_copy(source, target, read_sem.at[n])
-        for n, (source, target, _, _, _) in enumerate(parts)
+        pltpu.make_async_copy(*part[0], read_sem.at[n]) for n, part in enumerate(parts)
     ]
-    writes = [
-        pltpu.make_async_copy(source, target, write_sem.at[n])
-        for n, (_, _, _, source, target) in enumerate(parts)
-    ]
+    writes = []
     for copy in reads:
         copy.start()
-    for copy, write, part in zip(reads, writes, parts):
+    for copy, (_, convert, results) in zip(reads, parts):
         copy.wait()
-        part[2]()
-        write.start()
+        convert()
+        for source, target in results:
+            writes.append(pltpu.make_async_copy(source, target, write_sem.at[len(writes)]))
+            writes[-1].start()
     for ref, row in zip(refs[7:16], (0, 1, 3, 4, 5, 6, 7, 8, 9)):
         for layer in range(LAYERS):
-            ref[pl.ds(layer, 1), :] = small[layer, pl.ds(row, 1), pl.ds(0, ref.shape[1])]
-    dim = f_act.shape[2]
-    count = small[0, pl.ds(13, 1), pl.ds(0, 1)]
+            ref[pl.ds(layer, 1), :] = small[pl.ds(layer * 16 + row, 1), pl.ds(0, ref.shape[1])]
+    count = small[pl.ds(13, 1), pl.ds(0, 1)]
     for layer in range(LAYERS):
-        sums = jnp.sum(small[layer, pl.ds(8, 8), pl.ds(0, dim)], axis=-1, keepdims=True)
+        sums = jnp.sum(small[pl.ds(layer * 16 + 8, 8), pl.ds(0, dim)], axis=-1, keepdims=True)
         for n in range(3):
             root_means[pl.ds(layer, 1), pl.ds(n, 1)] = jnp.sqrt(
                 sums[2 + n : 3 + n, :] / (count * dim)
@@ -1312,32 +1262,29 @@
     hidden = up_weight.shape[-1]
     head_dim = dim // HEADS
     f32, bf16 = jnp.float32, jnp.bfloat16
-    groups = GROUPS
     vmem = pl.BlockSpec(memory_space=pltpu.VMEM)
     hbm = pl.BlockSpec(memory_space=pl.ANY)
     smem = pl.BlockSpec(memory_space=pltpu.SMEM)
     block = (block_tables, local, dim)
     dma = pltpu.SemaphoreType.DMA
-    in_part = (LAYERS, groups, dim, 3 * dim // groups)
+    in_parts = [(groups, dim, 3 * dim // groups) for groups in GROUPS]
+    mid = (LAYERS, 3 * dim, dim)
     shards = 8 * row_parts // 2
 
     def received(shape):
-        lead, (height, width) = shape[:-2], shape[-2:]
-        return [
-            [pltpu.VMEM(lead + (height // n, width), bf16) for n in (2, 4, 8)]
-            + [pltpu.VMEM(lead + (3 * height // shards, width), bf16)]
-        ]
+        height = shape[-2]
+        return pltpu.VMEM(shape[:-2] + (height - height // shards, shape[-1]), bf16)
 
     act, xgrad, *sums, small = pl.pallas_call(
         functools.partial(table_kernel, local, block_tables, seq),
         out_shape=(
             jax.ShapeDtypeStruct(block, bf16),
             jax.ShapeDtypeStruct(block, bf16),
-            jax.ShapeDtypeStruct(in_part, bf16),
-            jax.ShapeDtypeStruct(out_weight.shape, bf16),
-            jax.ShapeDtypeStruct(up_weight.shape, bf16),
+            jax.ShapeDtypeStruct(in_parts[0], bf16),
+            jax.ShapeDtypeStruct(in_parts[1], bf16),
+            jax.ShapeDtypeStruct(mid, bf16),
             jax.ShapeDtypeStruct(down_weight.shape, bf16),
-            jax.ShapeDtypeStruct((LAYERS, 16, hidden), f32),
+            jax.ShapeDtypeStruct((LAYERS * 16, hidden), f32),
         ),
         in_specs=[hbm, hbm, smem, smem] + [hbm] * 4 + [vmem] * VECTORS,
         out_specs=(hbm,) * 6 + (vmem,),
@@ -1347,11 +1294,11 @@
             pltpu.VMEM(up_weight.shape, bf16),
             pltpu.VMEM(down_weight.shape, bf16),
             pltpu.VMEM((LAYERS * VECTORS, hidden), f32),
-            pltpu.VMEM(in_part, bf16),
-            pltpu.VMEM(out_weight.shape, bf16),
-            pltpu.VMEM(up_weight.shape, bf16),
+            pltpu.VMEM(in_parts[0], bf16),
+            pltpu.VMEM(in_parts[1], bf16),
+            pltpu.VMEM(mid, bf16),
             pltpu.VMEM(down_weight.shape, bf16),
-            pltpu.VMEM((LAYERS, 16, hidden), f32),
+            pltpu.VMEM((LAYERS * 16, hidden), f32),
             pltpu.VMEM((LAYERS, rows, dim), bf16),
             pltpu.VMEM((rows, dim), bf16),
             pltpu.VMEM((rows, dim), f32),
@@ -1370,35 +1317,31 @@
             pltpu.VMEM((seq, 1), f32),
             pltpu.VMEM((rows, 1), f32),
             pltpu.VMEM((rows, dim), bf16),
-            pltpu.VMEM((rows, hidden), bf16),
-            pltpu.VMEM((rows, dim), bf16),
             pltpu.VMEM((rows, dim), bf16),
             pltpu.VMEM((8, rows), f32),
-            pltpu.VMEM((dim, rows), f32),
-            pltpu.VMEM((2, rows, 2 * dim // groups), f32),
-            pltpu.VMEM((LAYERS, groups, rows, 2 * dim // groups), bf16),
-            pltpu.VMEM((LAYERS, groups, rows, 2 * dim // groups), bf16),
-            pltpu.VMEM((groups, rows, 3 * dim // groups), bf16),
+            pltpu.VMEM((rows, 2 * dim), bf16),
+            *[pltpu.VMEM((groups, rows, 2 * dim // groups), bf16) for groups in GROUPS],
+            pltpu.VMEM((rows, 3 * dim), bf16),
             pltpu.VMEM((2, rows, dim), bf16),
         ]
-        + received(in_part)
-        + received(out_weight.shape)
-        + received(up_weight.shape)
-        + received(down_weight.shape)
+        + [received(shape) for shape in (in_parts[0], in_parts[1], mid, down_weight.shape)]
         + [
-            [pltpu.VMEM((LAYERS, 16, hidden // n), f32) for n in (2, 4, 8)]
-            + [pltpu.VMEM((LAYERS, 3, 16, hidden // 8), f32)]
+            [
+                pltpu.VMEM((1, LAYERS * 16, hidden // 2), f32),
+                pltpu.VMEM((3, LAYERS * 16, hidden // 8), f32),
+                pltpu.VMEM((3, LAYERS * 16, hidden // 8), f32),
+            ]
         ]
         + [dma((block_tables,))] * 8
         + [
             dma((8,)),
             dma((LAYERS, HEADS, 2)),
-            dma((LAYERS, groups, 2)),
+            dma((LAYERS, HEADS, 2)),
             dma((2,)),
-            dma((LAYERS * (2 * HALVES + 2 + groups), 12)),
+            dma((LAYERS * (1 + HALVES) + sum(GROUPS) + 1, 12)),
         ],
         compiler_params=pltpu.CompilerParams(
-            collective_id=0, has_side_effects=True, vmem_limit_bytes=62 * 1024 * 1024
+            collective_id=0, has_side_effects=True, vmem_limit_bytes=63 * 1024 * 1024
         ),
     )(
         jnp.swapaxes(tables_in, 0, 1),
@@ -1437,18 +1380,21 @@
         out_specs=[hbm] * 6 + [vmem] * 10,
         scratch_shapes=[
             pltpu.VMEM(shape, dtype)
-            for dtype, in_shape, rows_shape in (
-                (bf16, in_part, block),
-                (f32, in_weight.shape, tables_in.shape),
-            )
-            for shape in (
-                rows_shape,
-                rows_shape,
-                in_shape,
-                out_weight.shape,
-                up_weight.shape,
-                down_weight.shape,
-            )
+            for dtype, shapes_of in (
+                (bf16, (block, block, *in_parts, mid, down_weight.shape)),
+                (
+                    f32,
+                    (
+                        tables_in.shape,
+                        tables_in.shape,
+                        in_weight.shape,
+                        out_weight.shape,
+                        up_weight.shape,
+                        down_weight.shape,
+                    ),
+                ),
+            )
+            for shape in shapes_of
         ]
         + [dma((5 * LAYERS + 2,))] * 2,
         compiler_params=pltpu.CompilerParams(vmem_limit_bytes=62 * 1024 * 1024),
@@ -1477,7 +1423,8 @@
 
 def per_device(tables, row_parts, *operands):
     local, block_tables, dim = operands[0].shape
-    if tables == 4 and row_parts == 2 * block_tables and local * row_parts <= 1024:
+    fits = local * row_parts <= 1024 and local * block_tables % TILE == 0
+    if tables == 4 and row_parts == 2 * block_tables and fits:
         return table_device(tables, row_parts, *operands)
     return gathered_device(*operands)
 

time: 161 us -> 153 us (0.950)
  Pallas kernels: 157 us -> 149 us
    pallas_call x1, Pallas kernels: 147 us -> 138 us  [table_device(): pl.pallas_call(functools.partial(table_kernel, local, block_tables, seq),...]
where the time goes in v5:
time: 153 us; the launch traced here: 152 us
  Pallas kernels  149 us (97%)
  local copies, waits for them, and re-layouts  2.37 us (2%)
    pallas_call x1, Pallas kernels, table_device(): pl.pallas_call(functools.partial(table_kernel, local, block_tables, seq),...  138 us
    pallas_call x1, Pallas kernels, table_device(): pl.pallas_call(widen_kernel, out_shape=shapes, in_specs=[hbm] * 6 + [vmem...  10.7 us

profile of v5, /device:TPU:0, one launch (start us, length us, event | category | flops | bytes accessed | tf_op | source)
XLA Modules:
  0.0 151.9 jit_solution(8601111441804933351)
XLA Ops:
  0.6 2.4 %copy_bitcast_fusion = (bf16[4,128,512]{2,1,0:T(8,128)(2,1)}, bf16[4,128,512]{2,1,0:T(8,128)(2,1)}) fusion(bf16[128,4,512]{2,1,0:T(4,128)(2,1)} %param.31, bf16[128,4,512]{2,1,0:T(4,128)(2,1)} %param.17), kind=kLoop, calls=%fused_computation | loop fusion | bytes 2097152 | tf_op jit(solution)/shard_map/transpose | solution.py:1348
  3.0 138.0 %shard_map.288 = (bf16[4,128,512]{2,1,0:T(8,128)(2,1)}, bf16[4,128,512]{2,1,0:T(8,128)(2,1)}, bf16[4,512,384]{2,1,0:T(8,128)(2,1)}, bf16[2,512,768]{2,1,0:T(8,12...) custom-call(bf16[4,128,512]{2,1,0:T(8,128)(2,1)} %get-tuple-element.63.x_hbm, ...), custom_call_target="tpu_custom_call" | custom-call | tf_op jit(solution)/shard_map/pallas_call | solution.py:1278
  141.0 10.7 %shard_map.289 = (f32[128,4,512]{2,1,0:T(4,128)}, f32[128,4,512]{2,1,0:T(4,128)}, f32[2,512,1536]{2,1,0:T(8,128)}, f32[2,512,512]{2,1,0:T(8,128)}, f32[2,512,102...) custom-call(bf16[4,512,384]{2,1,0:T(8,128)(2,1)} %get-tuple-element., ...), custom_call_target="tpu_custom_call" | custom-call | tf_op jit(solution)/shard_map/pallas_call | solution.py:1376

commit v6 on v5

--- a/solution.py
+++ b/solution.py
@@ -828,13 +828,10 @@
 
     def forward(layer):
         def project(at):
-            projected = dot(in_low[layer, at, :], w_in[layer])
-            queries[layer, at, :] = (
-                (projected[:, :dim] + vector(0, layer, dim)) * scale
-            ).astype(jnp.bfloat16)
+            projected = dot(in_low[layer, at, :], w_in[layer, :, pl.ds(dim, 2 * dim)])
             own = pl.ds(pl.multiple_of(own_rows + at.start, TILE), TILE)
-            key_rows = projected[:, dim : 2 * dim].astype(jnp.bfloat16)
-            value_rows = (projected[:, 2 * dim :] + vector(1, layer, dim)).astype(jnp.bfloat16)
+            key_rows = projected[:, :dim].astype(jnp.bfloat16)
+            value_rows = (projected[:, dim:] + vector(1, layer, dim)).astype(jnp.bfloat16)
             for h in range(HEADS):
                 cols = slice(h * head_dim, (h + 1) * head_dim)
                 kv[layer, h, own, pl.ds(0, head_dim)] = key_rows[:, cols]
@@ -848,6 +845,14 @@
 
         for h in range(HEADS):
             kv_copy(h).start()
+
+        def ask(at):
+            projected = dot(in_low[layer, at, :], w_in[layer, :, pl.ds(0, dim)])
+            queries[layer, at, :] = ((projected + vector(0, layer, dim)) * scale).astype(
+                jnp.bfloat16
+            )
+
+        each_tile(ask)
 
         def attend(h, carry):
             cols = head_cols(h)

time: 153 us -> 152 us (level)
  no operation moved by 1% of the time
where the time goes in v6:
time: 152 us; the launch traced here: 151 us
  Pallas kernels  148 us (97%)
  local copies, waits for them, and re-layouts  2.37 us (2%)
    pallas_call x1, Pallas kernels, table_device(): pl.pallas_call(functools.partial(table_kernel, local, block_tables, seq),...  137 us
    pallas_call x1, Pallas kernels, table_device(): pl.pallas_call(widen_kernel, out_shape=shapes, in_specs=[hbm] * 6 + [vmem...  10.7 us

profile of v6, /device:TPU:0, one launch (start us, length us, event | category | flops | bytes accessed | tf_op | source)
XLA Modules:
  0.0 151.4 jit_solution(8316369002712780009)
XLA Ops:
  0.6 2.4 %copy_bitcast_fusion = (bf16[4,128,512]{2,1,0:T(8,128)(2,1)}, bf16[4,128,512]{2,1,0:T(8,128)(2,1)}) fusion(bf16[128,4,512]{2,1,0:T(4,128)(2,1)} %param.31, bf16[128,4,512]{2,1,0:T(4,128)(2,1)} %param.17), kind=kLoop, calls=%fused_computation | loop fusion | bytes 2097152 | tf_op jit(solution)/shard_map/transpose | solution.py:1353
  3.0 137.5 %shard_map.288 = (bf16[4,128,512]{2,1,0:T(8,128)(2,1)}, bf16[4,128,512]{2,1,0:T(8,128)(2,1)}, bf16[4,512,384]{2,1,0:T(8,128)(2,1)}, bf16[2,512,768]{2,1,0:T(8,12...) custom-call(bf16[4,128,512]{2,1,0:T(8,128)(2,1)} %get-tuple-element.63.x_hbm, ...), custom_call_target="tpu_custom_call" | custom-call | tf_op jit(solution)/shard_map/pallas_call | solution.py:1283
  140.5 10.7 %shard_map.289 = (f32[128,4,512]{2,1,0:T(4,128)}, f32[128,4,512]{2,1,0:T(4,128)}, f32[2,512,1536]{2,1,0:T(8,128)}, f32[2,512,512]{2,1,0:T(8,128)}, f32[2,512,102...) custom-call(bf16[4,512,384]{2,1,0:T(8,128)(2,1)} %get-tuple-element., ...), custom_call_target="tpu_custom_call" | custom-call | tf_op jit(solution)/shard_map/pallas_call | solution.py:1381
